TPU v7x, 128 devices: a whole 4x4x4 slice. The times are simulated.
128 devices in a mesh: gx: 16 (over y, x), gy: 8 (over z, core).
Axes of the slice: x: 4, y: 4, z: 4, core: 2. Of those that a mesh axis runs over, the one named last changes fastest.
Arguments:
- melt_field: float32 [4096, 256, 256], P('gx', 'gy'), may hold values from -90 to 90
- start_time: float32 [256, 32], replicated, may hold values from -6 to 6
- start_x: float32 [4096, 256], P('gx'), may hold values from -6 to 6
Outputs:
- time_basis: float32 [256, 32], replicated
- x_basis: float32 [4096, 256], P('gx')
- core: float32 [256, 8192], P('gx', 'gy')
All inputs are finite; a program needn't handle non-finite values.
Results may differ from a plain program's by a relative error of at most 0.0003.
Values sent between devices are 32-bit elements; how exact they have to be, the bound alone decides.
No kernel may reach another device: no remote copies, remote signals or barrier semaphores. Data moves between devices by JAX's collectives and lax.ppermute only.
A program may use at most 128 MiB of HBM per device.

v0:
```python
import jax
import jax.numpy as jnp
from jax import lax
from jax.sharding import PartitionSpec as P

ITERS_T = 8
SWEEPS_X = 3


def precise_dot(left, right):
    return jnp.dot(left, right, precision=lax.Precision.HIGHEST, preferred_element_type=jnp.float32)


def inner_dot(left, right):
    return lax.dot_general(
        left,
        right,
        (((0,), (0,)), ((), ())),
        precision=lax.Precision.HIGHEST,
        preferred_element_type=jnp.float32,
    )


def orthonormal(applied, cross_prod):
    factor = jnp.linalg.cholesky(cross_prod)
    return lax.linalg.triangular_solve(
        factor, applied, left_side=False, lower=True, transpose_a=True
    )


def refine(applied):
    cross_prod = lax.psum(inner_dot(applied, applied), "gx")
    return orthonormal(applied, cross_prod)


def local(melt_field, start_time, start_x):
    cells_x, cells_y, time_len = melt_field.shape
    flattened = melt_field.reshape(cells_x * cells_y, time_len)
    gram_time = lax.psum(inner_dot(flattened, flattened), ("gx", "gy"))
    time_basis = start_time
    for repeat in range(ITERS_T):
        applied = precise_dot(gram_time, time_basis)
        time_basis = orthonormal(applied, inner_dot(applied, applied))
    shrunk = precise_dot(flattened, time_basis).reshape(cells_x, cells_y * time_basis.shape[1])
    basis_x = start_x
    gram_partial = lax.dot_general(
        shrunk,
        lax.all_gather(shrunk, "gx", axis=0, tiled=True),
        (((1,), (1,)), ((), ())),
        precision=lax.Precision.HIGHEST,
        preferred_element_type=jnp.float32,
    )
    gram_full = lax.psum(gram_partial, "gy")
    for repeat in range(SWEEPS_X):
        gathered = lax.all_gather(basis_x, "gx", axis=0, tiled=True)
        applied = precise_dot(gram_full, gathered)
        basis_x = refine(applied)
    core = lax.psum_scatter(inner_dot(basis_x, shrunk), "gx", scatter_dimension=0, tiled=True)
    return (time_basis, basis_x, core)


def solution(mesh):
    in_specs = (P("gx", "gy", None), P(), P("gx", None))
    out_specs = (P(), P("gx", None), P("gx", "gy"))
    return jax.shard_map(local, mesh=mesh, in_specs=in_specs, out_specs=out_specs, check_vma=False)
```

profile of v0, /device:TPU:0, one launch (start us, length us, event | category | flops | bytes accessed | tf_op | source)
XLA Modules:
  0.0 1163.0 jit_solution(9058660879889650622)
XLA Ops:
  7.2 17.7 %convolution_bitcast_fusion.1 = f32[256,256]{1,0:T(8,128)} fusion(f32[256,32,256]{2,1,0:T(8,128)} %param.9), kind=kOutput, calls=%fused_computation.7 | convolution fusion | flops 6442450944 | bytes 8650752 | tf_op jit(solution)/shard_map/dot_general | solution.py:15
  25.3 144.2 %all-reduce.7.cloned.1.call-done = f32[256,256]{1,0:T(8,128)} async-done(((f32[256,256]{1,0:T(8,128)}), f32[256,256]{1,0:T(8,128)}) %all-reduce.7.cloned.1.call-update) | async-done | bytes 262160 | tf_op jit(solution)/shard_map/psum | solution.py:39
  236.7 10.4 convolution_bitcast_fusion
  255.1 107.6 %all-gather.5.cloned.1.call-done = f32[4096,1024]{1,0:T(8,128)} async-done(((f32[256,1024]{1,0:T(8,128)}), f32[4096,1024]{1,0:T(8,128)}) %all-gather.5.cloned.1.call-update) | async-done | bytes 16777232 | tf_op jit(solution)/shard_map/all_gather | solution.py:48
  362.7 18.3 %fusion.90 = f32[256,4096]{1,0:T(8,128)} fusion(f32[256,1024]{1,0:T(8,128)} %reshape.41, f32[4096,1024]{1,0:T(8,128)} %all-gather.5.cloned.1.call-done), kind=kOutput, calls=%fused_computation.175 | convolution fusion | flops 12884901888 | bytes 22020096 | tf_op jit(solution)/shard_map/dot_general | solution.py:46
  381.1 34.9 %all-gather.7.cloned.1.call-done = f32[4096,256]{1,0:T(8,128)} async-done(((f32[256,256]{1,0:T(8,128)}), f32[4096,256]{1,0:T(8,128)}) %all-gather.7.cloned.1.call-update) | async-done | bytes 4194320 | tf_op jit(solution)/shard_map/all_gather | solution.py:55
  416.0 74.8 %all-reduce.9.cloned.1.call-done = f32[256,4096]{1,0:T(8,128)} async-done(((f32[256,4096]{1,0:T(8,128)}), f32[256,4096]{1,0:T(8,128)}) %all-reduce.9.cloned.1.call-update) | async-done | bytes 4194320 | tf_op jit(solution)/shard_map/psum | solution.py:53
  499.4 83.8 %all-reduce.11.cloned.1.call-done = f32[256,256]{0,1:T(8,128)} async-done(((f32[256,256]{0,1:T(8,128)}), f32[256,256]{0,1:T(8,128)}) %all-reduce.11.cloned.1.call-update) | async-done | bytes 262160 | tf_op jit(solution)/shard_map/psum | solution.py:32
  585.3 11.7 %cholesky.392 = f32[128,128]{1,0:T(8,128)S(1)} custom-call(f32[128,128]{1,0:T(8,128)S(1)} %cholesky.490), custom_call_target="Cholesky" | custom-call | tf_op jit(solution)/shard_map/jit(cholesky)/cholesky | solution.py:25
  607.4 11.7 %cholesky.409 = f32[128,128]{1,0:T(8,128)S(1)} custom-call(f32[128,128]{1,0:T(8,128)S(1)} %convolution_subtract_fusion.5), custom_call_target="Cholesky" | custom-call | tf_op jit(solution)/shard_map/jit(cholesky)/cholesky | solution.py:25
  625.3 19.7 %custom-call.36 = f32[2,128,128]{1,2,0:T(8,128)S(1)} custom-call(f32[2,128,128]{2,1,0:T(8,128)S(1)} %get-tuple-element.27), custom_call_target="InvertDiagBlocksLowerTriangular" | custom-call | tf_op jit(solution)/shard_map/triangular_solve/custom-call.5 | solution.py:26
  646.9 56.9 %all-gather.9.cloned.1.call-done = f32[4096,256]{0,1:T(8,128)} async-done(((f32[256,256]{0,1:T(8,128)}), f32[4096,256]{0,1:T(8,128)}) %all-gather.9.cloned.1.call-update) | async-done | bytes 4194320 | tf_op jit(solution)/shard_map/all_gather | solution.py:55
  703.8 11.4 fusion.93
  716.9 83.3 %all-reduce.13.cloned.1.call-done = f32[256,256]{0,1:T(8,128)} async-done(((f32[256,256]{0,1:T(8,128)}), f32[256,256]{0,1:T(8,128)}) %all-reduce.13.cloned.1.call-update) | async-done | bytes 262160 | tf_op jit(solution)/shard_map/psum | solution.py:32
  802.2 11.7 %cholesky.426 = f32[128,128]{1,0:T(8,128)S(1)} custom-call(f32[128,128]{1,0:T(8,128)S(1)} %cholesky.493), custom_call_target="Cholesky" | custom-call | tf_op jit(solution)/shard_map/jit(cholesky)/cholesky | solution.py:25
  824.3 11.7 %cholesky.443 = f32[128,128]{1,0:T(8,128)S(1)} custom-call(f32[128,128]{1,0:T(8,128)S(1)} %convolution_subtract_fusion.4), custom_call_target="Cholesky" | custom-call | tf_op jit(solution)/shard_map/jit(cholesky)/cholesky | solution.py:25
  843.1 19.7 %custom-call.38 = f32[2,128,128]{1,2,0:T(8,128)S(1)} custom-call(f32[2,128,128]{2,1,0:T(8,128)S(1)} %get-tuple-element.28), custom_call_target="InvertDiagBlocksLowerTriangular" | custom-call | tf_op jit(solution)/shard_map/triangular_solve/custom-call.5 | solution.py:26
  864.6 56.9 %all-gather.11.cloned.1.call-done = f32[4096,256]{0,1:T(8,128)} async-done(((f32[256,256]{0,1:T(8,128)}), f32[4096,256]{0,1:T(8,128)}) %all-gather.11.cloned.1.call-update) | async-done | bytes 4194320 | tf_op jit(solution)/shard_map/all_gather | solution.py:55
  921.5 11.4 fusion.95
  934.5 83.4 %all-reduce.15.cloned.1.call-done = f32[256,256]{0,1:T(8,128)} async-done(((f32[256,256]{0,1:T(8,128)}), f32[256,256]{0,1:T(8,128)}) %all-reduce.15.cloned.1.call-update) | async-done | bytes 262160 | tf_op jit(solution)/shard_map/psum | solution.py:32
  1020.0 11.7 %cholesky.460 = f32[128,128]{1,0:T(8,128)S(1)} custom-call(f32[128,128]{1,0:T(8,128)S(1)} %cholesky.496), custom_call_target="Cholesky" | custom-call | tf_op jit(solution)/shard_map/jit(cholesky)/cholesky | solution.py:25
  1042.1 11.7 %cholesky.477 = f32[128,128]{1,0:T(8,128)S(1)} custom-call(f32[128,128]{1,0:T(8,128)S(1)} %convolution_subtract_fusion.3), custom_call_target="Cholesky" | custom-call | tf_op jit(solution)/shard_map/jit(cholesky)/cholesky | solution.py:25
  1060.9 19.7 %custom-call.40 = f32[2,128,128]{1,2,0:T(8,128)S(1)} custom-call(f32[2,128,128]{2,1,0:T(8,128)S(1)} %get-tuple-element.29), custom_call_target="InvertDiagBlocksLowerTriangular" | custom-call | tf_op jit(solution)/shard_map/triangular_solve/custom-call.5 | solution.py:26
  1084.5 71.4 %reduce-scatter.2.cloned.1.call-done = f32[16,1024]{1,0:T(8,128)} async-done(((f32[256,1024]{1,0:T(8,128)}), f32[16,1024]{1,0:T(8,128)}) %reduce-scatter.2.cloned.1.call-update) | async-done | bytes 65552 | tf_op jit(solution)/shard_map/reduce_scatter | solution.py:58
  (189 shorter events, 160.0 us)
Async XLA Ops:
  7.2 162.4 %copy-start = (f32[256,32]{0,1:T(8,128)S(1)}, f32[256,32]{0,1:T(8,128)}, u32[]{:S(2)}) copy-start(f32[256,32]{0,1:T(8,128)} %param.10) | copy-start | bytes 98308
  7.2 162.4 %all-reduce.7.cloned.1.call-start = ((), (), s32[]{:S(2)}) async-start(), calls=%async_computation.1 | async-start | bytes 524288 | tf_op jit(solution)/shard_map/psum | solution.py:39
  25.0 337.7 %all-gather.5.cloned.1.call-start = ((), (), s32[]{:S(2)}) async-start(), calls=%async_computation.2 | async-start | bytes 17825792 | tf_op jit(solution)/shard_map/all_gather | solution.py:48
  169.6 59.5 %copy-start.1 = (f32[256,256]{1,0:T(8,128)S(1)}, f32[256,256]{1,0:T(8,128)}, u32[]{:S(2)}) copy-start(f32[256,256]{1,0:T(8,128)} %all-reduce.7.cloned.1.call-done) | copy-start | bytes 786436
  236.7 10.4 copy-start.3
  254.3 161.7 %all-gather.7.cloned.1.call-start = ((), (), s32[]{:S(2)}) async-start(), calls=%async_computation.4 | async-start | bytes 4456448 | tf_op jit(solution)/shard_map/all_gather | solution.py:55
  255.1 235.7 %all-reduce.9.cloned.1.call-start = ((), (), s32[]{:S(2)}) async-start(), calls=%async_computation.3 | async-start | bytes 8388608 | tf_op jit(solution)/shard_map/psum | solution.py:53
  381.1 202.1 %all-reduce.11.cloned.1.call-start = ((), (), s32[]{:S(2)}) async-start(), calls=%async_computation.5 | async-start | bytes 524288 | tf_op jit(solution)/shard_map/psum | solution.py:32
  499.2 204.6 %all-gather.9.cloned.1.call-start = ((), (), s32[]{:S(2)}) async-start(), calls=%async_computation.6 | async-start | bytes 4456448 | tf_op jit(solution)/shard_map/all_gather | solution.py:55
  646.8 153.3 %all-reduce.13.cloned.1.call-start = ((), (), s32[]{:S(2)}) async-start(), calls=%async_computation.7 | async-start | bytes 524288 | tf_op jit(solution)/shard_map/psum | solution.py:32
  716.6 205.0 %all-gather.11.cloned.1.call-start = ((), (), s32[]{:S(2)}) async-start(), calls=%async_computation.8 | async-start | bytes 4456448 | tf_op jit(solution)/shard_map/all_gather | solution.py:55
  864.5 153.4 %all-reduce.15.cloned.1.call-start = ((), (), s32[]{:S(2)}) async-start(), calls=%async_computation.9 | async-start | bytes 524288 | tf_op jit(solution)/shard_map/psum | solution.py:32
  933.0 148.7 %copy-start.2 = (f32[256,1024]{1,0:T(8,128)S(1)}, f32[256,1024]{1,0:T(8,128)}, u32[]{:S(2)}) copy-start(f32[256,1024]{1,0:T(8,128)} %reshape.41) | copy-start | bytes 3145732
  934.3 221.6 %reduce-scatter.2.cloned.1.call-start = ((), (), s32[]{:S(2)}) async-start(), calls=%async_computation.10 | async-start | bytes 1114112 | tf_op jit(solution)/shard_map/reduce_scatter | solution.py:58
Sparse Core Ops, SparseCore 0:
  25.1 144.4 all-reduce.6
  254.5 108.2 all-gather.4
  364.9 51.1 all-gather.6
  418.3 72.5 all-reduce.8
  499.3 83.8 all-reduce.10
  646.9 56.8 all-gather.8
  716.7 83.4 all-reduce.12
  864.7 56.8 all-gather.10
  934.4 83.4 all-reduce.14
  1083.8 72.1 reduce-scatter.1
where the time goes:
time: 1170 us; the launch traced here: 1160 us
  waiting for transfers between devices  798 us (68%)
  other arithmetic  220 us (19%)
  matrix products  99.5 us (9%)
  local copies, waits for them, and re-layouts  23.9 us (2%)
  between operations  18.9 us (2%)
    psum x3, waiting for transfers between devices, refine(): cross_prod = lax.psum(inner_dot(applied, applied), 'gx')  250 us
    all_gather x3, waiting for transfers between devices, local(): gathered = lax.all_gather(basis_x, 'gx', axis=0, tiled=True)  149 us
    psum x1, waiting for transfers between devices, local(): gram_time = lax.psum(inner_dot(flattened, flattened), ('gx', 'gy'))  144 us
    another operation x44, other arithmetic, orthonormal(): factor = jnp.linalg.cholesky(cross_prod)  132 us
    all_gather x1, waiting for transfers between devices, local(): lax.all_gather(shrunk, 'gx', axis=0, tiled=True)  108 us
    another operation x26, other arithmetic, orthonormal(): lax.linalg.triangular_solve(factor, applied, left_side=False, lower=True,...  85.3 us
    psum x1, waiting for transfers between devices, local(): gram_full = lax.psum(gram_partial, 'gy')  74.8 us
    reduce_scatter x1, waiting for transfers between devices, local(): lax.psum_scatter(inner_dot(basis_x, shrunk), 'gx', scatter_dimension=0, t...  71.4 us
  transfers between devices with their start and end apart: 10, of which 10 were waited for; matrix products, arithmetic and copies ran while one was open for 2% of the time, Pallas kernels for 0%

commit v1 on v0

v1 whole, which is shorter than its diff:
```python
import functools

import jax
import jax.numpy as jnp
from jax import lax
from jax.experimental import pallas as pl
from jax.experimental.pallas import tpu as pltpu
from jax.sharding import PartitionSpec as P

ITERS_T = 8
SWEEPS_X = 3
F32 = jnp.float32
BF16 = jnp.bfloat16
HI = lax.Precision.HIGHEST


def split3(x):
    h = x.astype(BF16)
    rest = x - h.astype(F32)
    m = rest.astype(BF16)
    l = (rest - m.astype(F32)).astype(BF16)
    return h, m, l


def split2(x):
    h = x.astype(BF16)
    return h, (x - h.astype(F32)).astype(BF16)


def dot(a, b, ca=1, cb=0):
    return lax.dot_general(a, b, (((ca,), (cb,)), ((), ())), preferred_element_type=F32)


def packed_rhs(b):
    h, m, l = b
    return jnp.concatenate([h, m, h, m, l, h], axis=0)


def packed_lhs(a, axis):
    h, m, l = a
    return jnp.concatenate([h, h, m, m, h, l], axis=axis)


def inverse_factor(gram):
    n = gram.shape[0]
    tiles = n // 8
    left = [gram[8 * t : 8 * t + 8] for t in range(tiles)]
    row_id = lax.broadcasted_iota(jnp.int32, (8, n), 0)
    col_id = lax.broadcasted_iota(jnp.int32, (8, n), 1)
    right = [jnp.where(col_id == row_id + 8 * t, 1.0, 0.0).astype(F32) for t in range(tiles)]
    out = []
    for b in range(tiles):
        cols = {
            t: [jnp.broadcast_to(left[t][:, 8 * b + m : 8 * b + m + 1], (8, n)) for m in range(8)]
            for t in range(b, tiles)
        }
        rows_l, rows_r = left[b], right[b]
        steps = []
        scale = jnp.ones((8, n), F32)
        for m in range(8):
            pivot = jnp.broadcast_to(cols[b][m][m : m + 1], (8, n))
            inv = 1.0 / pivot
            scale = jnp.where(row_id == m, lax.rsqrt(pivot), scale)
            factor = {t: cols[t][m] * inv for t in range(b, tiles)}
            factor[b] = jnp.where(row_id > m, factor[b], 0.0)
            for n2 in range(m + 1, 8):
                value = jnp.broadcast_to(cols[b][n2][m : m + 1], (8, n))
                for t in range(b, tiles):
                    cols[t][n2] = cols[t][n2] - factor[t] * value
            row_l = jnp.broadcast_to(rows_l[m : m + 1], (8, n))
            row_r = jnp.broadcast_to(rows_r[m : m + 1], (8, n))
            rows_l = rows_l - factor[b] * row_l
            rows_r = rows_r - factor[b] * row_r
            steps.append((factor, row_l, row_r))
        for t in range(b + 1, tiles):
            for factor, row_l, row_r in steps:
                left[t] = left[t] - factor[t] * row_l
                right[t] = right[t] - factor[t] * row_r
        out.append(rows_r * scale)
    return jnp.concatenate(out, axis=0)


BLK = 32


def chol_kernel(c_ref, out_ref, work):
    n = c_ref.shape[0]
    col_id = lax.broadcasted_iota(jnp.int32, (BLK, n), 1)
    row_id = lax.broadcasted_iota(jnp.int32, (BLK, n), 0)
    work[...] = c_ref[...]
    diag = work[0:BLK, 0:BLK]
    for k in range(n // BLK):
        lo, hi = k * BLK, (k + 1) * BLK
        inv = inverse_factor(diag)
        in_blk = (col_id >= lo) & (col_id < hi)
        row = jnp.where(in_blk, jnp.where(col_id - lo == row_id, 1.0, 0.0), work[lo:hi, :])
        r = dot(packed_lhs(split3(inv), 1), packed_rhs(split3(row)))
        out_ref[lo:hi, :] = jnp.where(col_id < hi, r, 0.0)
        if hi < n:
            parts = split3(r)
            xt, w = packed_lhs(parts, 0), packed_rhs(parts)
            small = dot(xt[:, hi : hi + BLK], w[:, hi : hi + BLK], 0, 0)
            diag = work[hi : hi + BLK, hi : hi + BLK] - small
            base = hi // 128 * 128
            upd = dot(xt[:, base:], w, 0, 0)
            cid = lax.broadcasted_iota(jnp.int32, (n - hi, n), 1)
            old = jnp.where((cid >= lo) & (cid < hi), 0.0, work[hi:, :])
            work[hi:, :] = old - upd[hi - base :, :]


def chol_inverse(c):
    n = c.shape[0]
    return pl.pallas_call(
        chol_kernel,
        out_shape=jax.ShapeDtypeStruct((n, n), F32),
        in_specs=[pl.BlockSpec(memory_space=pltpu.VMEM)],
        out_specs=pl.BlockSpec(memory_space=pltpu.VMEM),
        scratch_shapes=[pltpu.VMEM((n, n), F32)],
        compiler_params=pltpu.CompilerParams(vmem_limit_bytes=16 << 20),
        cost_estimate=pl.CostEstimate(flops=1 << 30, bytes_accessed=1 << 20, transcendentals=0),
    )(c)


def gram_kernel(m_ref, out_ref, high, cross, low):
    step = pl.program_id(0)

    @pl.when(step == 0)
    def _():
        high[...] = jnp.zeros_like(high)
        cross[...] = jnp.zeros_like(cross)
        low[...] = jnp.zeros_like(low)

    h, l = split2(m_ref[...])
    high[...] += dot(h, h, 0, 0)
    cross[...] += dot(h, l, 0, 0)
    low[...] += dot(l, l, 0, 0)

    @pl.when(step == pl.num_programs(0) - 1)
    def _():
        c = cross[...]
        out_ref[...] = high[...] + (c + c.T + low[...])


def time_gram(field):
    rows, n = field.shape
    block = 1024
    return pl.pallas_call(
        gram_kernel,
        grid=(rows // block,),
        out_shape=jax.ShapeDtypeStruct((n, n), F32),
        in_specs=[pl.BlockSpec((block, n), lambda i: (i, 0))],
        out_specs=pl.BlockSpec((n, n), lambda i: (0, 0)),
        scratch_shapes=[pltpu.VMEM((n, n), F32)] * 3,
        compiler_params=pltpu.CompilerParams(vmem_limit_bytes=24 << 20),
    )(field)


def time_steps(g_ref, s_ref, gs):
    gs[0], gs[1], gs[2] = split3(g_ref[...])
    z0 = s_ref[...].T
    n = z0.shape[0]

    def apply_g(z):
        h, m, l = split3(z)
        a = dot(jnp.concatenate([h, m, l], axis=0), gs[0])
        b = dot(jnp.concatenate([h, m], axis=0), gs[1])
        c = dot(h, gs[2])
        return a[:n] + ((a[n : 2 * n] + b[:n]) + ((a[2 * n :] + b[n:]) + c))

    def gram(z):
        parts = jnp.concatenate(split3(z), axis=0)
        a = dot(parts, parts, 1, 1)
        two = a[:n, n : 2 * n] + a[n : 2 * n, :n]
        three = a[n : 2 * n, n : 2 * n] + (a[:n, 2 * n :] + a[2 * n :, :n])
        return a[:n, :n] + (two + three)

    def step(_, z):
        y = apply_g(z)
        inv = inverse_factor(gram(z))
        return dot(packed_lhs(split3(inv), 1), packed_rhs(split3(y)))

    z = lax.fori_loop(0, ITERS_T - 1, step, apply_g(z0))
    inv = inverse_factor(gram(z))
    return dot(packed_lhs(split3(inv), 1), packed_rhs(split3(z))).T


def project_kernel(g_ref, s_ref, u_ref, m_hbm, q_ref, shrunk_ref, v_ref, gs, m_left, m_right, weights, sems):
    rows, n = m_hbm.shape
    lanes = 128
    copies = [
        pltpu.make_async_copy(m_hbm.at[:, pl.ds(i * lanes, lanes)], half, sems.at[i])
        for i, half in enumerate((m_left, m_right))
    ]
    for copy in copies:
        copy.start()
    q = time_steps(g_ref, s_ref, gs)
    q_ref[...] = q
    rank = q.shape[1]
    per = lanes // rank
    qh, ql = split2(q)
    qh, ql = qh.astype(F32), ql.astype(F32)
    for k in range(per):
        pad = lambda a: jnp.pad(a, ((0, 0), (k * rank, lanes - (k + 1) * rank)))
        weights[k] = jnp.concatenate([pad(qh), pad(ql)], axis=1).astype(BF16)
    for copy in copies:
        copy.wait()
    cells_x = shrunk_ref.shape[0]
    cells_y = rows // cells_x
    for group in range(cells_y // per):
        wide = jnp.zeros((cells_x, 2 * lanes), F32)
        thin = jnp.zeros((cells_x, lanes), F32)
        for k in range(per):
            at = pl.ds(group * per + k, cells_x, stride=cells_y)
            h, l = split2(jnp.concatenate([m_left[at, :], m_right[at, :]], axis=1))
            wide = wide + dot(h, weights[k])
            thin = thin + dot(l, weights[k, :, :lanes])
        shrunk_ref[:, group * lanes : (group + 1) * lanes] = wide[:, :lanes] + (wide[:, lanes:] + thin)
    v_ref[...] = jnp.dot(u_ref[...].T, shrunk_ref[...], precision=HI, preferred_element_type=F32)


def project(gram, start_time, start_x, field, cells_x):
    rows, n = field.shape
    rank = start_time.shape[1]
    cols = rows // cells_x * rank
    vmem = pl.BlockSpec(memory_space=pltpu.VMEM)
    return pl.pallas_call(
        project_kernel,
        out_shape=(
            jax.ShapeDtypeStruct((n, rank), F32),
            jax.ShapeDtypeStruct((cells_x, cols), F32),
            jax.ShapeDtypeStruct((start_x.shape[1], cols), F32),
        ),
        in_specs=[vmem, vmem, vmem, pl.BlockSpec(memory_space=pl.ANY)],
        out_specs=(vmem, vmem, vmem),
        scratch_shapes=[
            pltpu.VMEM((3, n, n), BF16),
            pltpu.VMEM((rows, n // 2), F32),
            pltpu.VMEM((rows, n // 2), F32),
            pltpu.VMEM((128 // rank, n, 256), BF16),
            pltpu.SemaphoreType.DMA((2,)),
        ],
        compiler_params=pltpu.CompilerParams(vmem_limit_bytes=40 << 20),
    )(gram, start_time, start_x, field)


def precise(a, b, cb):
    return lax.dot_general(a, b, (((1,), (cb,)), ((), ())), precision=HI, preferred_element_type=F32)


def scatter_sum(v, axis, size):
    parts = v.reshape((size, v.shape[0] // size) + v.shape[1:])
    return jnp.sum(lax.all_to_all(parts, axis, 0, 0, tiled=True), axis=0)


def spread(p, axis, size):
    copies = jnp.broadcast_to(p[None], (size,) + p.shape)
    got = lax.all_to_all(copies, axis, 0, 0, tiled=True)
    return got.reshape((size * p.shape[0],) + p.shape[1:])


def sum_gy(z, size):
    ring = size // 2
    swap = [(2 * k + c, 2 * k + 1 - c) for k in range(ring) for c in range(2)]
    turn = lambda d: [(2 * k + c, 2 * ((k + d) % ring) + c) for k in range(ring) for c in range(2)]
    core = lax.axis_index("gy") % 2
    half = z.shape[0] // 2
    mine = lax.dynamic_slice_in_dim(z, core * half, half, 0)
    other = lax.dynamic_slice_in_dim(z, (1 - core) * half, half, 0)
    mine = mine + lax.ppermute(other, "gy", swap)
    total = (mine + lax.ppermute(mine, "gy", turn(2))) + (
        lax.ppermute(mine, "gy", turn(1)) + lax.ppermute(mine, "gy", turn(3))
    )
    rest = lax.ppermute(total, "gy", swap)
    first = core == 0
    return jnp.concatenate([jnp.where(first, total, rest), jnp.where(first, rest, total)], axis=0)


def local(melt_field, start_time, start_x, *, gx, gy):
    cells_x, cells_y, time_len = melt_field.shape
    field = melt_field.reshape(cells_x * cells_y, time_len)
    both = ("gx", "gy")
    gram = spread(scatter_sum(time_gram(field), both, gx * gy), both, gx * gy)
    time_basis, shrunk, v = project(gram, start_time, start_x, field, cells_x)
    cols = shrunk.shape[1]
    v = spread(scatter_sum(v, "gx", gx), "gx", gx)
    z = sum_gy(precise(v, shrunk, 1), gy)
    for sweep in range(SWEEPS_X - 1):
        vc = jnp.concatenate([precise(z, shrunk, 0), precise(z, z, 1)], axis=1)
        vc = spread(scatter_sum(vc, "gx", gx), "gx", gx)
        inv = chol_inverse(vc[:, cols:])
        z = precise(inv, sum_gy(precise(vc[:, :cols], shrunk, 1), gy), 0)
    inv = chol_inverse(spread(scatter_sum(precise(z, z, 1), "gx", gx), "gx", gx))
    u = precise(inv, z, 0)
    core = scatter_sum(precise(u, shrunk, 0), "gx", gx)
    return (time_basis, u.T, core)


def solution(mesh):
    in_specs = (P("gx", "gy", None), P(), P("gx", None))
    out_specs = (P(), P("gx", None), P("gx", "gy"))
    body = functools.partial(local, gx=mesh.shape["gx"], gy=mesh.shape["gy"])
    return jax.shard_map(body, mesh=mesh, in_specs=in_specs, out_specs=out_specs, check_vma=False)
```

time: 1170 us -> 334 us (0.29)
  waiting for transfers between devices: 798 us -> 67.1 us
  other arithmetic: 220 us -> 1.47 us
  blocking collectives: 0 us -> 158 us
  matrix products: 99.5 us -> 9.56 us
  Pallas kernels: 0 us -> 58.1 us
  starting transfers between devices: 1.3 us -> 23.8 us
  between operations: 18.9 us -> 1.23 us
  local copies, waits for them, and re-layouts: 23.9 us -> 10.9 us
    psum x5 -> x0, waiting for transfers between devices: 469 us -> none  [the longest x3 250 us: refine(): cross_prod = lax.psum(inner_dot(applied, applied), 'gx')]
    all_gather x4 -> x0, waiting for transfers between devices: 256 us -> none  [the longest x3 149 us: local(): gathered = lax.all_gather(basis_x, 'gx', axis=0, tiled=True)]
    another operation x70 -> x0, other arithmetic: 217 us -> none  [the longest x44 132 us: orthonormal(): factor = jnp.linalg.cholesky(cross_prod)]
    all_to_all x0 -> x8, blocking collectives: none -> 158 us  [the longest x5 101 us: scatter_sum(): return jnp.sum(lax.all_to_all(parts, axis, 0, 0, tiled=True), axis=0)]
    dot_general x26 -> x12, matrix products: 93 us -> 9.56 us  [precise(): lax.dot_general(a, b, (((1,), (cb,)), ((), ())), precision=HI, preferred_...]
    reduce_scatter x1 -> x0, waiting for transfers between devices: 71.4 us -> none  [local(): lax.psum_scatter(inner_dot(basis_x, shrunk), 'gx', scatter_dimension=0, t...]
    pallas_call x0 -> x5, Pallas kernels: none -> 58.1 us  [the longest x3 29.8 us: chol_inverse(): pl.pallas_call(chol_kernel, out_shape=jax.ShapeDtypeStruct((n, n), F32),...]
    all_to_all x0 -> x3, waiting for transfers between devices: none -> 41.7 us  [the longest x2 27.2 us: spread(): got = lax.all_to_all(copies, axis, 0, 0, tiled=True)]
  transfers between devices with their start and end apart: 10 -> 18, of which waited for: 10 -> 13; matrix products, arithmetic and copies ran while one was open for 2% -> 1% of each run, Pallas kernels for 0% -> 6%
where the time goes in v1:
time: 334 us; the launch traced here: 330 us
  blocking collectives  158 us (47%)
  waiting for transfers between devices  67.1 us (20%)
  Pallas kernels  58.1 us (17%)
  starting transfers between devices  23.8 us (7%)
  local copies, waits for them, and re-layouts  10.9 us (3%)
  matrix products  9.56 us (3%)
    all_to_all x5, blocking collectives, scatter_sum(): return jnp.sum(lax.all_to_all(parts, axis, 0, 0, tiled=True), axis=0)  101 us
    all_to_all x3, blocking collectives, spread(): got = lax.all_to_all(copies, axis, 0, 0, tiled=True)  56.7 us
    pallas_call x3, Pallas kernels, chol_inverse(): pl.pallas_call(chol_kernel, out_shape=jax.ShapeDtypeStruct((n, n), F32),...  29.8 us
    all_to_all x2, waiting for transfers between devices, spread(): got = lax.all_to_all(copies, axis, 0, 0, tiled=True)  27.2 us
    pallas_call x1, Pallas kernels, project(): pl.pallas_call(project_kernel, out_shape=(jax.ShapeDtypeStruct((n, rank),...  23 us
    all_to_all x1, waiting for transfers between devices, scatter_sum(): return jnp.sum(lax.all_to_all(parts, axis, 0, 0, tiled=True), axis=0)  14.4 us
    ppermute x3, waiting for transfers between devices, sum_gy(): lax.ppermute(mine, 'gy', turn(1)) + lax.ppermute(mine, 'gy', turn(3))  12.7 us
    dot_general x12, matrix products, precise(): lax.dot_general(a, b, (((1,), (cb,)), ((), ())), precision=HI, preferred_...  9.56 us
  transfers between devices with their start and end apart: 18, of which 13 were waited for; matrix products, arithmetic and copies ran while one was open for 1% of the time, Pallas kernels for 6%

profile of v1, /device:TPU:0, one launch (start us, length us, event | category | flops | bytes accessed | tf_op | source)
XLA Modules:
  0.0 329.9 jit_solution(16624978876191536462)
XLA Ops:
  0.6 3.4 %copy-done = f32[256,32,256]{2,1,0:T(8,128)S(1)} copy-done((f32[256,32,256]{2,1,0:T(8,128)S(1)}, f32[256,32,256]{2,1,0:T(8,128)}, u32[]{:S(2)}) %copy-start) | copy-done | bytes 8388632
  4.0 5.2 %shard_map.58 = f32[256,256]{1,0:T(8,128)S(1)} custom-call(f32[8192,256]{1,0:T(8,128)S(1)} %bitcast.28), custom_call_target="tpu_custom_call" | custom-call | tf_op jit(solution)/shard_map/pallas_call | solution.py:147
  9.4 21.9 %all_to_all.55 = f32[128,2,256]{2,1,0:T(2,128)S(1)} all-to-all(f32[128,2,256]{2,1,0:T(2,128)S(1)} %reshape.48), channel_id=1, replica_groups=mesh['gx'=16,'gy'=8] {'gx','gy'}, dimensions={0} | all-to-all | bytes 524288 | tf_op jit(solution)/shard_map/all_to_all | solution.py:252
  32.2 4.6 %all-to-all-start.1 = ((f32[128,2,256]{2,1,0:T(2,128)}), f32[128,2,256]{2,1,0:T(2,128)S(1)}, u32[]{:S(2)}, u32[]{:S(2)}) async-start(f32[128,2,256]{2,1,0:T(2,128)} %broadcast_in_dim.10), calls=%async_computation.1 | async-start | bytes 524288 | tf_op jit(solution)/shard_map/all_to_all | solution.py:257
  37.0 10.8 %all-to-all-done.1 = f32[128,2,256]{2,1,0:T(2,128)S(1)} async-done(((f32[128,2,256]{2,1,0:T(2,128)}), f32[128,2,256]{2,1,0:T(2,128)S(1)}, u32[]{:S(2)}, u32[]{:S(2)}) %all-to-all-start.1) | async-done | bytes 262176 | tf_op jit(solution)/shard_map/all_to_all | solution.py:257
  48.0 3.4 %copy-done.1 = f32[256,32,256]{2,1,0:T(8,128)S(1)} copy-done((f32[256,32,256]{2,1,0:T(8,128)S(1)}, f32[256,32,256]{2,1,0:T(8,128)}, u32[]{:S(2)}) %copy-start.1) | copy-done | bytes 8388632
  51.4 23.0 %shard_map.59 = (f32[256,32]{1,0:T(8,128)S(1)}, f32[256,1024]{1,0:T(8,128)S(1)}, f32[256,1024]{1,0:T(8,128)S(1)}) custom-call(f32[256,256]{1,0:T(8,128)S(1)} %reshape.49.g_ref, f32[256,32]{1,0:T(8,128)S(1)} %copy.6.s_ref, f32[256,256]{1,0:T(8,128)S(1)} %copy-done.2, f32[8192,256]{1,0:T(8,128)S(1)} %bitcast.29), custom_call_target="tpu_custom_call" | custom-call | tf_op jit(solution)/shard_map/pallas_call | solution.py:226
  74.4 20.1 %all_to_all.56 = f32[16,16,1024]{2,1,0:T(8,128)S(1)} all-to-all(f32[16,16,1024]{2,1,0:T(8,128)S(1)} %bitcast.30), channel_id=1, replica_groups=mesh['gx'=16,'gy'=8] {'gx'}, dimensions={0} | all-to-all | bytes 2097152 | tf_op jit(solution)/shard_map/all_to_all | solution.py:252
  95.6 3.9 %all-to-all-start.3 = ((f32[16,16,1024]{2,1,0:T(8,128)}), f32[16,16,1024]{2,1,0:T(8,128)S(1)}, u32[]{:S(2)}, u32[]{:S(2)}) async-start(f32[16,16,1024]{2,1,0:T(8,128)} %broadcast_in_dim.11), calls=%async_computation.3 | async-start | bytes 2097152 | tf_op jit(solution)/shard_map/all_to_all | solution.py:257
  99.5 16.4 %all-to-all-done.3 = f32[16,16,1024]{2,1,0:T(8,128)S(1)} async-done(((f32[16,16,1024]{2,1,0:T(8,128)}), f32[16,16,1024]{2,1,0:T(8,128)S(1)}, u32[]{:S(2)}, u32[]{:S(2)}) %all-to-all-start.3) | async-done | bytes 1048608 | tf_op jit(solution)/shard_map/all_to_all | solution.py:257
  124.4 4.3 %collective-permute-done.2 = f32[128,256]{1,0:T(8,128)S(1)} collective-permute-done((f32[128,256]{1,0:T(8,128)S(1)}, f32[128,256]{1,0:T(8,128)S(1)}, u32[]{:S(2)}, u32[]{:S(2)}) %collective-permute-start.2) | collective-permute-done | bytes 131104 | tf_op jit(solution)/shard_map/ppermute | solution.py:271
  131.8 23.3 %all_to_all.57 = f32[16,16,1280]{2,1,0:T(8,128)S(1)} all-to-all(f32[16,16,1280]{2,1,0:T(8,128)S(1)} %bitcast.36), channel_id=1, replica_groups=mesh['gx'=16,'gy'=8] {'gx'}, dimensions={0} | all-to-all | bytes 2621440 | tf_op jit(solution)/shard_map/all_to_all | solution.py:252
  155.2 22.6 %all_to_all.58 = f32[16,16,1280]{2,1,0:T(8,128)S(1)} all-to-all(f32[16,16,1280]{2,1,0:T(8,128)S(1)} %broadcast_in_dim.12), channel_id=1, replica_groups=mesh['gx'=16,'gy'=8] {'gx'}, dimensions={0} | all-to-all | bytes 2621440 | tf_op jit(solution)/shard_map/all_to_all | solution.py:257
  186.4 4.0 %collective-permute-done.7 = f32[128,256]{1,0:T(8,128)S(1)} collective-permute-done((f32[128,256]{1,0:T(8,128)S(1)}, f32[128,256]{1,0:T(8,128)S(1)}, u32[]{:S(2)}, u32[]{:S(2)}) %collective-permute-start.7) | collective-permute-done | bytes 131104 | tf_op jit(solution)/shard_map/ppermute | solution.py:271
  191.0 9.9 %shard_map.60 = f32[256,256]{1,0:T(8,128)S(1)} custom-call(f32[256,256]{1,0:T(8,128)S(1)} %slice.16.c_ref), custom_call_target="tpu_custom_call" | custom-call | flops 1073741824 | bytes 1048576 | tf_op jit(solution)/shard_map/pallas_call | solution.py:113
  202.9 23.6 %all_to_all.59 = f32[16,16,1280]{2,1,0:T(8,128)S(1)} all-to-all(f32[16,16,1280]{2,1,0:T(8,128)S(1)} %bitcast.37), channel_id=1, replica_groups=mesh['gx'=16,'gy'=8] {'gx'}, dimensions={0} | all-to-all | bytes 2621440 | tf_op jit(solution)/shard_map/all_to_all | solution.py:252
  226.7 22.5 %all_to_all.60 = f32[16,16,1280]{2,1,0:T(8,128)S(1)} all-to-all(f32[16,16,1280]{2,1,0:T(8,128)S(1)} %broadcast_in_dim.13), channel_id=1, replica_groups=mesh['gx'=16,'gy'=8] {'gx'}, dimensions={0} | all-to-all | bytes 2621440 | tf_op jit(solution)/shard_map/all_to_all | solution.py:257
  257.6 4.4 %collective-permute-done.12 = f32[128,256]{1,0:T(8,128)S(1)} collective-permute-done((f32[128,256]{1,0:T(8,128)S(1)}, f32[128,256]{1,0:T(8,128)S(1)}, u32[]{:S(2)}, u32[]{:S(2)}) %collective-permute-start.12) | collective-permute-done | bytes 131104 | tf_op jit(solution)/shard_map/ppermute | solution.py:271
  262.4 9.9 %shard_map.61 = f32[256,256]{1,0:T(8,128)S(1)} custom-call(f32[256,256]{1,0:T(8,128)S(1)} %slice.18.c_ref), custom_call_target="tpu_custom_call" | custom-call | flops 1073741824 | bytes 1048576 | tf_op jit(solution)/shard_map/pallas_call | solution.py:113
  273.2 12.2 %all_to_all.61 = f32[16,16,256]{2,1,0:T(8,128)S(1)} all-to-all(f32[16,16,256]{2,1,0:T(8,128)S(1)} %bitcast.40), channel_id=1, replica_groups=mesh['gx'=16,'gy'=8] {'gx'}, dimensions={0} | all-to-all | bytes 524288 | tf_op jit(solution)/shard_map/all_to_all | solution.py:252
  285.5 11.6 %all_to_all.62 = f32[16,16,256]{2,1,0:T(8,128)S(1)} all-to-all(f32[16,16,256]{2,1,0:T(8,128)S(1)} %broadcast_in_dim.14), channel_id=1, replica_groups=mesh['gx'=16,'gy'=8] {'gx'}, dimensions={0} | all-to-all | bytes 524288 | tf_op jit(solution)/shard_map/all_to_all | solution.py:257
  297.1 9.9 %shard_map.62 = f32[256,256]{1,0:T(8,128)S(1)} custom-call(f32[256,256]{1,0:T(8,128)S(1)} %bitcast.31), custom_call_target="tpu_custom_call" | custom-call | flops 1073741824 | bytes 1048576 | tf_op jit(solution)/shard_map/pallas_call | solution.py:113
  309.4 3.7 %all-to-all-start.10 = ((f32[16,16,1024]{2,1,0:T(8,128)}), f32[16,16,1024]{2,1,0:T(8,128)S(1)}, u32[]{:S(2)}, u32[]{:S(2)}) async-start(f32[16,16,1024]{2,1,0:T(8,128)} %bitcast.10), calls=%async_computation.10 | async-start | bytes 2097152 | tf_op jit(solution)/shard_map/all_to_all | solution.py:252
  314.6 14.4 %all-to-all-done.10 = f32[16,16,1024]{2,1,0:T(8,128)S(1)} async-done(((f32[16,16,1024]{2,1,0:T(8,128)}), f32[16,16,1024]{2,1,0:T(8,128)S(1)}, u32[]{:S(2)}, u32[]{:S(2)}) %all-to-all-start.10) | async-done | bytes 1048608 | tf_op jit(solution)/shard_map/all_to_all | solution.py:252
  (77 shorter events, 39.6 us)
Async XLA Ops:
  0.6 3.4 %copy-start = (f32[256,32,256]{2,1,0:T(8,128)S(1)}, f32[256,32,256]{2,1,0:T(8,128)}, u32[]{:S(2)}) copy-start(f32[256,32,256]{2,1,0:T(8,128)} %param.3) | copy-start | bytes 25165828
  9.3 27.6 %copy-start.3 = (f32[256,32]{0,1:T(8,128)S(1)}, f32[256,32]{0,1:T(8,128)}, u32[]{:S(2)}) copy-start(f32[256,32]{0,1:T(8,128)} %param.4) | copy-start | bytes 98308
  9.3 38.7 %copy-start.2 = (f32[256,256]{1,0:T(8,128)S(1)}, f32[256,256]{1,0:T(8,128)}, u32[]{:S(2)}) copy-start(f32[256,256]{1,0:T(8,128)} %u_ref.1) | copy-start | bytes 786436
  32.2 15.6 %all-to-all-start.1 = ((f32[128,2,256]{2,1,0:T(2,128)}), f32[128,2,256]{2,1,0:T(2,128)S(1)}, u32[]{:S(2)}, u32[]{:S(2)}) async-start(f32[128,2,256]{2,1,0:T(2,128)} %broadcast_in_dim.10), calls=%async_computation.1 | async-start | bytes 524288 | tf_op jit(solution)/shard_map/all_to_all | solution.py:257
  48.0 3.4 %copy-start.1 = (f32[256,32,256]{2,1,0:T(8,128)S(1)}, f32[256,32,256]{2,1,0:T(8,128)}, u32[]{:S(2)}) copy-start(f32[256,32,256]{2,1,0:T(8,128)} %param.3) | copy-start | bytes 25165828
  95.6 20.3 %all-to-all-start.3 = ((f32[16,16,1024]{2,1,0:T(8,128)}), f32[16,16,1024]{2,1,0:T(8,128)S(1)}, u32[]{:S(2)}, u32[]{:S(2)}) async-start(f32[16,16,1024]{2,1,0:T(8,128)} %broadcast_in_dim.11), calls=%async_computation.3 | async-start | bytes 2097152 | tf_op jit(solution)/shard_map/all_to_all | solution.py:257
  117.0 1.4 collective-permute-start
  118.5 6.0 %collective-permute-start.3 = (f32[128,256]{1,0:T(8,128)S(1)}, f32[128,256]{1,0:T(8,128)S(1)}, u32[]{:S(2)}, u32[]{:S(2)}) collective-permute-start(f32[128,256]{1,0:T(8,128)S(1)} %dynamic-slice_add_fusion.2), channel_id=1, source_target_pairs={{0,6},{1,7},{2,0},{3,1},{4,2},{5,3},{6,4},{7,5},{8,14},{9,15},{10,... | collective-permute-start | bytes 393224 | tf_op jit(solution)/shard_map/ppermute | solution.py:271
  119.4 9.3 %collective-permute-start.2 = (f32[128,256]{1,0:T(8,128)S(1)}, f32[128,256]{1,0:T(8,128)S(1)}, u32[]{:S(2)}, u32[]{:S(2)}) collective-permute-start(f32[128,256]{1,0:T(8,128)S(1)} %dynamic-slice_add_fusion.2), channel_id=1, source_target_pairs={{0,2},{1,3},{2,4},{3,5},{4,6},{5,7},{6,0},{7,1},{8,10},{9,11},{10,... | collective-permute-start | bytes 393224 | tf_op jit(solution)/shard_map/ppermute | solution.py:271
  120.6 8.1 %collective-permute-start.1 = (f32[128,256]{1,0:T(8,128)S(1)}, f32[128,256]{1,0:T(8,128)S(1)}, u32[]{:S(2)}, u32[]{:S(2)}) collective-permute-start(f32[128,256]{1,0:T(8,128)S(1)} %dynamic-slice_add_fusion.2), channel_id=1, source_target_pairs={{0,4},{1,5},{2,6},{3,7},{4,0},{5,1},{6,2},{7,3},{8,12},{9,13},{10,... | collective-permute-start | bytes 393224 | tf_op jit(solution)/shard_map/ppermute | solution.py:270
  128.7 1.4 collective-permute-start.4
  178.8 1.4 collective-permute-start.5
  180.3 6.1 %collective-permute-start.8 = (f32[128,256]{1,0:T(8,128)S(1)}, f32[128,256]{1,0:T(8,128)S(1)}, u32[]{:S(2)}, u32[]{:S(2)}) collective-permute-start(f32[128,256]{1,0:T(8,128)S(1)} %dynamic-slice_add_fusion.1), channel_id=1, source_target_pairs={{0,6},{1,7},{2,0},{3,1},{4,2},{5,3},{6,4},{7,5},{8,14},{9,15},{10,... | collective-permute-start | bytes 393224 | tf_op jit(solution)/shard_map/ppermute | solution.py:271
  181.1 9.3 %collective-permute-start.7 = (f32[128,256]{1,0:T(8,128)S(1)}, f32[128,256]{1,0:T(8,128)S(1)}, u32[]{:S(2)}, u32[]{:S(2)}) collective-permute-start(f32[128,256]{1,0:T(8,128)S(1)} %dynamic-slice_add_fusion.1), channel_id=1, source_target_pairs={{0,2},{1,3},{2,4},{3,5},{4,6},{5,7},{6,0},{7,1},{8,10},{9,11},{10,... | collective-permute-start | bytes 393224 | tf_op jit(solution)/shard_map/ppermute | solution.py:271
  182.4 8.0 %collective-permute-start.6 = (f32[128,256]{1,0:T(8,128)S(1)}, f32[128,256]{1,0:T(8,128)S(1)}, u32[]{:S(2)}, u32[]{:S(2)}) collective-permute-start(f32[128,256]{1,0:T(8,128)S(1)} %dynamic-slice_add_fusion.1), channel_id=1, source_target_pairs={{0,4},{1,5},{2,6},{3,7},{4,0},{5,1},{6,2},{7,3},{8,12},{9,13},{10,... | collective-permute-start | bytes 393224 | tf_op jit(solution)/shard_map/ppermute | solution.py:270
  190.5 10.5 %collective-permute-start.9 = (f32[128,256]{1,0:T(8,128)S(1)}, f32[128,256]{1,0:T(8,128)S(1)}, u32[]{:S(2)}, u32[]{:S(2)}) collective-permute-start(f32[128,256]{1,0:T(8,128)S(1)} %add_add_fusion.1), channel_id=1, source_target_pairs={{0,1},{1,0},{2,3},{3,2},{4,5},{5,4},{6,7},{7,6},{8,9},{9,8},{10,11... | collective-permute-start | bytes 393224 | tf_op jit(solution)/shard_map/ppermute | solution.py:273
  250.3 1.4 collective-permute-start.10
  251.7 5.9 %collective-permute-start.13 = (f32[128,256]{1,0:T(8,128)S(1)}, f32[128,256]{1,0:T(8,128)S(1)}, u32[]{:S(2)}, u32[]{:S(2)}) collective-permute-start(f32[128,256]{1,0:T(8,128)S(1)} %dynamic-slice_add_fusion), channel_id=1, source_target_pairs={{0,6},{1,7},{2,0},{3,1},{4,2},{5,3},{6,4},{7,5},{8,14},{9,15},{10,... | collective-permute-start | bytes 393224 | tf_op jit(solution)/shard_map/ppermute | solution.py:271
  252.8 9.3 %collective-permute-start.12 = (f32[128,256]{1,0:T(8,128)S(1)}, f32[128,256]{1,0:T(8,128)S(1)}, u32[]{:S(2)}, u32[]{:S(2)}) collective-permute-start(f32[128,256]{1,0:T(8,128)S(1)} %dynamic-slice_add_fusion), channel_id=1, source_target_pairs={{0,2},{1,3},{2,4},{3,5},{4,6},{5,7},{6,0},{7,1},{8,10},{9,11},{10,... | collective-permute-start | bytes 393224 | tf_op jit(solution)/shard_map/ppermute | solution.py:271
  253.8 8.2 %collective-permute-start.11 = (f32[128,256]{1,0:T(8,128)S(1)}, f32[128,256]{1,0:T(8,128)S(1)}, u32[]{:S(2)}, u32[]{:S(2)}) collective-permute-start(f32[128,256]{1,0:T(8,128)S(1)} %dynamic-slice_add_fusion), channel_id=1, source_target_pairs={{0,4},{1,5},{2,6},{3,7},{4,0},{5,1},{6,2},{7,3},{8,12},{9,13},{10,... | collective-permute-start | bytes 393224 | tf_op jit(solution)/shard_map/ppermute | solution.py:270
  262.1 10.2 %collective-permute-start.14 = (f32[128,256]{1,0:T(8,128)S(1)}, f32[128,256]{1,0:T(8,128)S(1)}, u32[]{:S(2)}, u32[]{:S(2)}) collective-permute-start(f32[128,256]{1,0:T(8,128)S(1)} %add_add_fusion), channel_id=1, source_target_pairs={{0,1},{1,0},{2,3},{3,2},{4,5},{5,4},{6,7},{7,6},{8,9},{9,8},{10,11... | collective-permute-start | bytes 393224 | tf_op jit(solution)/shard_map/ppermute | solution.py:273
  309.4 19.6 %all-to-all-start.10 = ((f32[16,16,1024]{2,1,0:T(8,128)}), f32[16,16,1024]{2,1,0:T(8,128)S(1)}, u32[]{:S(2)}, u32[]{:S(2)}) async-start(f32[16,16,1024]{2,1,0:T(8,128)} %bitcast.10), calls=%async_computation.10 | async-start | bytes 2097152 | tf_op jit(solution)/shard_map/all_to_all | solution.py:252

commit v2 on v1

--- a/solution.py
+++ b/solution.py
@@ -29,16 +29,6 @@
 
 def dot(a, b, ca=1, cb=0):
     return lax.dot_general(a, b, (((ca,), (cb,)), ((), ())), preferred_element_type=F32)
-
-
-def packed_rhs(b):
-    h, m, l = b
-    return jnp.concatenate([h, m, h, m, l, h], axis=0)
-
-
-def packed_lhs(a, axis):
-    h, m, l = a
-    return jnp.concatenate([h, h, m, m, h, l], axis=axis)
 
 
 def inverse_factor(gram):
@@ -48,36 +38,61 @@
     row_id = lax.broadcasted_iota(jnp.int32, (8, n), 0)
     col_id = lax.broadcasted_iota(jnp.int32, (8, n), 1)
     right = [jnp.where(col_id == row_id + 8 * t, 1.0, 0.0).astype(F32) for t in range(tiles)]
+    bc = lambda x, m: jnp.broadcast_to(x[m : m + 1], (8, n))
+    lane = lambda x, j: jnp.broadcast_to(x[:, j : j + 1], (8, n))
     out = []
+    cols = {(t, j): lane(left[t], j) for j in range(8) for t in range(tiles)}
     for b in range(tiles):
-        cols = {
-            t: [jnp.broadcast_to(left[t][:, 8 * b + m : 8 * b + m + 1], (8, n)) for m in range(8)]
-            for t in range(b, tiles)
-        }
+        for j in range(8 * b + 8, min(8 * b + 16, n)):
+            for t in range(b + 1, tiles):
+                cols[t, j] = lane(left[t], j)
         rows_l, rows_r = left[b], right[b]
         steps = []
-        scale = jnp.ones((8, n), F32)
-        for m in range(8):
-            pivot = jnp.broadcast_to(cols[b][m][m : m + 1], (8, n))
-            inv = 1.0 / pivot
-            scale = jnp.where(row_id == m, lax.rsqrt(pivot), scale)
-            factor = {t: cols[t][m] * inv for t in range(b, tiles)}
-            factor[b] = jnp.where(row_id > m, factor[b], 0.0)
-            for n2 in range(m + 1, 8):
-                value = jnp.broadcast_to(cols[b][n2][m : m + 1], (8, n))
-                for t in range(b, tiles):
-                    cols[t][n2] = cols[t][n2] - factor[t] * value
-            row_l = jnp.broadcast_to(rows_l[m : m + 1], (8, n))
-            row_r = jnp.broadcast_to(rows_r[m : m + 1], (8, n))
-            rows_l = rows_l - factor[b] * row_l
-            rows_r = rows_r - factor[b] * row_r
-            steps.append((factor, row_l, row_r))
+        pivots = jnp.ones((8, n), F32)
+        for m in range(0, 8, 2):
+            c = 8 * b + m
+            a, d, e = bc(cols[b, c], m), bc(cols[b, c + 1], m + 1), bc(cols[b, c + 1], m)
+            ra = 1.0 / a
+            ratio = e * ra
+            rd = a * (1.0 / (a * d - e * e))
+            pivots = jnp.where(row_id == m, a, jnp.where(row_id == m + 1, d - e * ratio, pivots))
+            f0 = {t: cols[t, c] * ra for t in range(b, tiles)}
+            f1 = {t: (cols[t, c + 1] - f0[t] * e) * rd for t in range(b, tiles)}
+            f0[b] = jnp.where(row_id > m, f0[b], 0.0)
+            f1[b] = jnp.where(row_id > m + 1, f1[b], 0.0)
+            for j in range(c + 2, min(8 * b + 16, n)):
+                tj, mj = j // 8, j % 8
+                v0 = bc(cols[b, j], m) if tj == b else bc(cols[tj, c], mj)
+                v1 = bc(cols[b, j], m + 1) if tj == b else bc(cols[tj, c + 1], mj)
+                v1 = v1 - ratio * v0
+                for t in range(tj, tiles):
+                    cols[t, j] = (cols[t, j] - f0[t] * v0) - f1[t] * v1
+            l0, r0 = bc(rows_l, m), bc(rows_r, m)
+            l1, r1 = bc(rows_l, m + 1) - ratio * l0, bc(rows_r, m + 1) - ratio * r0
+            rows_l = (rows_l - f0[b] * l0) - f1[b] * l1
+            rows_r = (rows_r - f0[b] * r0) - f1[b] * r1
+            steps += [(f0, l0, r0), (f1, l1, r1)]
         for t in range(b + 1, tiles):
             for factor, row_l, row_r in steps:
                 left[t] = left[t] - factor[t] * row_l
                 right[t] = right[t] - factor[t] * row_r
-        out.append(rows_r * scale)
+        out.append(rows_r * lax.rsqrt(pivots))
     return jnp.concatenate(out, axis=0)
+
+
+def dot6(a, b, ca=1, cb=0):
+    n = a.shape[0]
+    h, m, l = split3(a)
+    x = dot(jnp.concatenate([h, m, l], axis=0), b[0], ca, cb)
+    y = dot(jnp.concatenate([h, m], axis=0), b[1], ca, cb)
+    z = dot(h, b[2], ca, cb)
+    return x[:n] + ((x[n : 2 * n] + y[:n]) + ((x[2 * n :] + y[n:]) + z))
+
+def gram6(z):
+    h, m, l = split3(z)
+    a = jnp.concatenate([h, h, m, m, h, l], axis=1)
+    b = jnp.concatenate([h, m, h, m, l, h], axis=1)
+    return dot(a, b, 1, 1)
 
 
 BLK = 32
@@ -91,16 +106,22 @@
     diag = work[0:BLK, 0:BLK]
     for k in range(n // BLK):
         lo, hi = k * BLK, (k + 1) * BLK
+        if hi < n:
+            right = split3(work[lo:hi, hi : hi + BLK])
+            below = work[hi : hi + BLK, lo:hi]
+            after = work[hi : hi + BLK, hi : hi + BLK]
+        in_blk = (col_id >= lo) & (col_id < hi)
+        row = split3(jnp.where(in_blk, jnp.where(col_id - lo == row_id, 1.0, 0.0), work[lo:hi, :]))
         inv = inverse_factor(diag)
-        in_blk = (col_id >= lo) & (col_id < hi)
-        row = jnp.where(in_blk, jnp.where(col_id - lo == row_id, 1.0, 0.0), work[lo:hi, :])
-        r = dot(packed_lhs(split3(inv), 1), packed_rhs(split3(row)))
+        if hi < n:
+            panel = dot6(below, split3(inv), 1, 1)
+            diag = after - dot6(panel, split3(dot6(inv, right)))
+        r = dot6(inv, row)
         out_ref[lo:hi, :] = jnp.where(col_id < hi, r, 0.0)
         if hi < n:
-            parts = split3(r)
-            xt, w = packed_lhs(parts, 0), packed_rhs(parts)
-            small = dot(xt[:, hi : hi + BLK], w[:, hi : hi + BLK], 0, 0)
-            diag = work[hi : hi + BLK, hi : hi + BLK] - small
+            h, m, l = split3(r)
+            xt = jnp.concatenate([h, h, m, m, h, l], axis=0)
+            w = jnp.concatenate([h, m, h, m, l, h], axis=0)
             base = hi // 128 * 128
             upd = dot(xt[:, base:], w, 0, 0)
             cid = lax.broadcasted_iota(jnp.int32, (n - hi, n), 1)
@@ -151,37 +172,22 @@
         in_specs=[pl.BlockSpec((block, n), lambda i: (i, 0))],
         out_specs=pl.BlockSpec((n, n), lambda i: (0, 0)),
         scratch_shapes=[pltpu.VMEM((n, n), F32)] * 3,
-        compiler_params=pltpu.CompilerParams(vmem_limit_bytes=24 << 20),
+        compiler_params=pltpu.CompilerParams(vmem_limit_bytes=56 << 20),
     )(field)
 
 
 def time_steps(g_ref, s_ref, gs):
     gs[0], gs[1], gs[2] = split3(g_ref[...])
-    z0 = s_ref[...].T
-    n = z0.shape[0]
 
     def apply_g(z):
-        h, m, l = split3(z)
-        a = dot(jnp.concatenate([h, m, l], axis=0), gs[0])
-        b = dot(jnp.concatenate([h, m], axis=0), gs[1])
-        c = dot(h, gs[2])
-        return a[:n] + ((a[n : 2 * n] + b[:n]) + ((a[2 * n :] + b[n:]) + c))
-
-    def gram(z):
-        parts = jnp.concatenate(split3(z), axis=0)
-        a = dot(parts, parts, 1, 1)
-        two = a[:n, n : 2 * n] + a[n : 2 * n, :n]
-        three = a[n : 2 * n, n : 2 * n] + (a[:n, 2 * n :] + a[2 * n :, :n])
-        return a[:n, :n] + (two + three)
+        return dot6(z, (gs[0], gs[1], gs[2]))
 
     def step(_, z):
         y = apply_g(z)
-        inv = inverse_factor(gram(z))
-        return dot(packed_lhs(split3(inv), 1), packed_rhs(split3(y)))
-
-    z = lax.fori_loop(0, ITERS_T - 1, step, apply_g(z0))
-    inv = inverse_factor(gram(z))
-    return dot(packed_lhs(split3(inv), 1), packed_rhs(split3(z))).T
+        return dot6(inverse_factor(gram6(z)), split3(y))
+
+    z = lax.fori_loop(0, ITERS_T - 1, step, apply_g(s_ref[...].T))
+    return dot6(inverse_factor(gram6(z)), split3(z)).T
 
 
 def project_kernel(g_ref, s_ref, u_ref, m_hbm, q_ref, shrunk_ref, v_ref, gs, m_left, m_right, weights, sems):
@@ -239,7 +245,7 @@
             pltpu.VMEM((128 // rank, n, 256), BF16),
             pltpu.SemaphoreType.DMA((2,)),
         ],
-        compiler_params=pltpu.CompilerParams(vmem_limit_bytes=40 << 20),
+        compiler_params=pltpu.CompilerParams(vmem_limit_bytes=56 << 20),
     )(gram, start_time, start_x, field)
 
 
@@ -258,37 +264,53 @@
     return got.reshape((size * p.shape[0],) + p.shape[1:])
 
 
-def sum_gy(z, size):
+def gy_moves(size):
     ring = size // 2
     swap = [(2 * k + c, 2 * k + 1 - c) for k in range(ring) for c in range(2)]
-    turn = lambda d: [(2 * k + c, 2 * ((k + d) % ring) + c) for k in range(ring) for c in range(2)]
+    turns = [[(2 * k + c, 2 * ((k + d) % ring) + c) for k in range(ring) for c in range(2)] for d in (1, 2, 3)]
+    return swap, turns
+
+
+def sum_gy_small(p, size):
+    swap, turns = gy_moves(size)
+    p = p + lax.ppermute(p, "gy", swap)
+    got = [lax.ppermute(p, "gy", turn) for turn in turns]
+    return (p + got[1]) + (got[0] + got[2])
+
+
+def sum_gy(z, size, square=None):
+    swap, turns = gy_moves(size)
     core = lax.axis_index("gy") % 2
     half = z.shape[0] // 2
     mine = lax.dynamic_slice_in_dim(z, core * half, half, 0)
     other = lax.dynamic_slice_in_dim(z, (1 - core) * half, half, 0)
     mine = mine + lax.ppermute(other, "gy", swap)
-    total = (mine + lax.ppermute(mine, "gy", turn(2))) + (
-        lax.ppermute(mine, "gy", turn(1)) + lax.ppermute(mine, "gy", turn(3))
-    )
+    inv = None
+    if square is not None:
+        mine, square = lax.optimization_barrier((mine, square))
+    got = [lax.ppermute(mine, "gy", turn) for turn in turns]
+    if square is not None:
+        got, inv = lax.optimization_barrier((got, chol_inverse(square)))
+    total = (mine + got[1]) + (got[0] + got[2])
     rest = lax.ppermute(total, "gy", swap)
     first = core == 0
-    return jnp.concatenate([jnp.where(first, total, rest), jnp.where(first, rest, total)], axis=0)
+    full = jnp.concatenate([jnp.where(first, total, rest), jnp.where(first, rest, total)], axis=0)
+    return full, inv
 
 
 def local(melt_field, start_time, start_x, *, gx, gy):
     cells_x, cells_y, time_len = melt_field.shape
     field = melt_field.reshape(cells_x * cells_y, time_len)
-    both = ("gx", "gy")
-    gram = spread(scatter_sum(time_gram(field), both, gx * gy), both, gx * gy)
+    gram = spread(sum_gy_small(scatter_sum(time_gram(field), "gx", gx), gy), "gx", gx)
     time_basis, shrunk, v = project(gram, start_time, start_x, field, cells_x)
     cols = shrunk.shape[1]
     v = spread(scatter_sum(v, "gx", gx), "gx", gx)
-    z = sum_gy(precise(v, shrunk, 1), gy)
+    z, _ = sum_gy(precise(v, shrunk, 1), gy)
     for sweep in range(SWEEPS_X - 1):
         vc = jnp.concatenate([precise(z, shrunk, 0), precise(z, z, 1)], axis=1)
         vc = spread(scatter_sum(vc, "gx", gx), "gx", gx)
-        inv = chol_inverse(vc[:, cols:])
-        z = precise(inv, sum_gy(precise(vc[:, :cols], shrunk, 1), gy), 0)
+        z, inv = sum_gy(precise(vc[:, :cols], shrunk, 1), gy, vc[:, cols:])
+        z = precise(inv, z, 0)
     inv = chol_inverse(spread(scatter_sum(precise(z, z, 1), "gx", gx), "gx", gx))
     u = precise(inv, z, 0)
     core = scatter_sum(precise(u, shrunk, 0), "gx", gx)

time: 334 us -> 308 us (0.922)
  waiting for transfers between devices: 67.1 us -> 57.8 us
  Pallas kernels: 58.1 us -> 49.3 us
  blocking collectives: 158 us -> 150 us
  local copies, waits for them, and re-layouts: 10.9 us -> 5.19 us
  starting transfers between devices: 23.8 us -> 29.5 us
    pallas_call x3, Pallas kernels: 29.8 us -> 21.2 us  [chol_inverse(): pl.pallas_call(chol_kernel, out_shape=jax.ShapeDtypeStruct((n, n), F32),...]
    all_to_all x5, blocking collectives: 101 us -> 93.2 us  [scatter_sum(): return jnp.sum(lax.all_to_all(parts, axis, 0, 0, tiled=True), axis=0)]
    ppermute x9 -> x13, waiting for transfers between devices: 20.1 us -> 13.3 us  [the longest x9 8.7 us: sum_gy(): got = [lax.ppermute(mine, 'gy', turn) for turn in turns]]
    ppermute x9 -> x13, starting transfers between devices: 10.6 us -> 17.1 us  [the longest x9 11.1 us: sum_gy(): got = [lax.ppermute(mine, 'gy', turn) for turn in turns]]
    unnamed x11, local copies, waits for them, and re-layouts: 8.39 us -> 2.99 us
    all_to_all x2, waiting for transfers between devices: 27.2 us -> 22.4 us  [spread(): got = lax.all_to_all(copies, axis, 0, 0, tiled=True)]
    pallas_call x1, Pallas kernels: 23 us -> 18.9 us  [project(): pl.pallas_call(project_kernel, out_shape=(jax.ShapeDtypeStruct((n, rank),...]
    pallas_call x1, Pallas kernels: 5.24 us -> 9.18 us  [time_gram(): pl.pallas_call(gram_kernel, grid=(rows // block,), out_shape=jax.ShapeDty...]
  transfers between devices with their start and end apart: 18 -> 22, of which waited for: 13 -> 15; matrix products, arithmetic and copies ran while one was open for 1% -> 1% of each run, Pallas kernels for 6% -> 5%
where the time goes in v2:
time: 308 us; the launch traced here: 304 us
  blocking collectives  150 us (49%)
  waiting for transfers between devices  57.8 us (19%)
  Pallas kernels  49.3 us (16%)
  starting transfers between devices  29.5 us (10%)
  matrix products  9.58 us (3%)
  local copies, waits for them, and re-layouts  5.19 us (2%)
    all_to_all x5, blocking collectives, scatter_sum(): return jnp.sum(lax.all_to_all(parts, axis, 0, 0, tiled=True), axis=0)  93.2 us
    all_to_all x3, blocking collectives, spread(): got = lax.all_to_all(copies, axis, 0, 0, tiled=True)  56.9 us
    all_to_all x2, waiting for transfers between devices, spread(): got = lax.all_to_all(copies, axis, 0, 0, tiled=True)  22.4 us
    pallas_call x3, Pallas kernels, chol_inverse(): pl.pallas_call(chol_kernel, out_shape=jax.ShapeDtypeStruct((n, n), F32),...  21.2 us
    pallas_call x1, Pallas kernels, project(): pl.pallas_call(project_kernel, out_shape=(jax.ShapeDtypeStruct((n, rank),...  18.9 us
    all_to_all x1, waiting for transfers between devices, scatter_sum(): return jnp.sum(lax.all_to_all(parts, axis, 0, 0, tiled=True), axis=0)  14.2 us
    ppermute x9, starting transfers between devices, sum_gy(): got = [lax.ppermute(mine, 'gy', turn) for turn in turns]  11.1 us
    dot_general x12, matrix products, precise(): lax.dot_general(a, b, (((1,), (cb,)), ((), ())), precision=HI, preferred_...  9.58 us
  transfers between devices with their start and end apart: 22, of which 15 were waited for; matrix products, arithmetic and copies ran while one was open for 1% of the time, Pallas kernels for 5%

profile of v2, /device:TPU:0, one launch (start us, length us, event | category | flops | bytes accessed | tf_op | source)
XLA Modules:
  0.0 304.0 jit_solution(7108181577737772545)
XLA Ops:
  0.6 9.2 %shard_map.58 = f32[256,256]{1,0:T(8,128)} custom-call(f32[8192,256]{1,0:T(8,128)} %bitcast.31), custom_call_target="tpu_custom_call" | custom-call | tf_op jit(solution)/shard_map/pallas_call | solution.py:168
  9.8 15.9 %all_to_all.55 = f32[16,16,256]{2,1,0:T(8,128)S(1)} all-to-all(f32[16,16,256]{2,1,0:T(8,128)} %bitcast.42), channel_id=1, replica_groups=mesh['gx'=16,'gy'=8] {'gx'}, dimensions={0} | all-to-all | bytes 524288 | tf_op jit(solution)/shard_map/all_to_all | solution.py:258
  27.0 4.0 %collective-permute-start.3 = (f32[16,256]{1,0:T(8,128)S(1)}, f32[16,256]{1,0:T(8,128)S(1)}, u32[]{:S(2)}, u32[]{:S(2)}) collective-permute-start(f32[16,256]{1,0:T(8,128)S(1)} %add.64), channel_id=1, source_target_pairs={{0,6},{1,7},{2,0},{3,1},{4,2},{5,3},{6,4},{7,5},{8,14},{9,15},{10,... | collective-permute-start | bytes 49160 | tf_op jit(solution)/shard_map/ppermute | solution.py:277
  32.9 3.1 %collective-permute-done.2 = f32[16,256]{1,0:T(8,128)S(1)} collective-permute-done((f32[16,256]{1,0:T(8,128)S(1)}, f32[16,256]{1,0:T(8,128)S(1)}, u32[]{:S(2)}, u32[]{:S(2)}) %collective-permute-start.2) | collective-permute-done | bytes 16416 | tf_op jit(solution)/shard_map/ppermute | solution.py:277
  37.1 3.7 %all-to-all-start.1 = ((f32[16,16,256]{2,1,0:T(8,128)}), f32[16,16,256]{2,1,0:T(8,128)S(1)}, u32[]{:S(2)}, u32[]{:S(2)}) async-start(f32[16,16,256]{2,1,0:T(8,128)} %broadcast_in_dim.10), calls=%async_computation.1 | async-start | bytes 524288 | tf_op jit(solution)/shard_map/all_to_all | solution.py:263
  41.5 7.9 %all-to-all-done.1 = f32[16,16,256]{2,1,0:T(8,128)S(1)} async-done(((f32[16,16,256]{2,1,0:T(8,128)}), f32[16,16,256]{2,1,0:T(8,128)S(1)}, u32[]{:S(2)}, u32[]{:S(2)}) %all-to-all-start.1) | async-done | bytes 262176 | tf_op jit(solution)/shard_map/all_to_all | solution.py:263
  50.1 18.9 %shard_map.59 = (f32[256,32]{1,0:T(8,128)}, f32[256,1024]{1,0:T(8,128)}, f32[256,1024]{1,0:T(8,128)}) custom-call(f32[256,256]{1,0:T(8,128)} %bitcast.41, f32[256,32]{1,0:T(8,128)} %copy.6.s_ref, f32[256,256]{1,0:T(8,128)} %u_ref.1, f32[8192,256]{1,0:T(8,128)} %bitcast.32), custom_call_target="tpu_custom_call" | custom-call | tf_op jit(solution)/shard_map/pallas_call | solution.py:232
  69.1 19.0 %all_to_all.56 = f32[16,16,1024]{2,1,0:T(8,128)S(1)} all-to-all(f32[16,16,1024]{2,1,0:T(8,128)} %bitcast.44), channel_id=1, replica_groups=mesh['gx'=16,'gy'=8] {'gx'}, dimensions={0} | all-to-all | bytes 2097152 | tf_op jit(solution)/shard_map/all_to_all | solution.py:258
  89.3 4.0 %all-to-all-start.3 = ((f32[16,16,1024]{2,1,0:T(8,128)}), f32[16,16,1024]{2,1,0:T(8,128)S(1)}, u32[]{:S(2)}, u32[]{:S(2)}) async-start(f32[16,16,1024]{2,1,0:T(8,128)} %broadcast_in_dim.11), calls=%async_computation.3 | async-start | bytes 2097152 | tf_op jit(solution)/shard_map/all_to_all | solution.py:263
  93.3 14.5 %all-to-all-done.3 = f32[16,16,1024]{2,1,0:T(8,128)S(1)} async-done(((f32[16,16,1024]{2,1,0:T(8,128)}), f32[16,16,1024]{2,1,0:T(8,128)S(1)}, u32[]{:S(2)}, u32[]{:S(2)}) %all-to-all-start.3) | async-done | bytes 1048608 | tf_op jit(solution)/shard_map/all_to_all | solution.py:263
  110.3 2.7 collective-permute-start.7
  116.1 6.2 %collective-permute-done.6 = f32[128,256]{1,0:T(8,128)S(1)} collective-permute-done((f32[128,256]{1,0:T(8,128)S(1)}, f32[128,256]{1,0:T(8,128)S(1)}, u32[]{:S(2)}, u32[]{:S(2)}) %collective-permute-start.6) | collective-permute-done | bytes 131104 | tf_op jit(solution)/shard_map/ppermute | solution.py:291
  125.3 23.2 %all_to_all.57 = f32[16,16,1280]{2,1,0:T(8,128)S(1)} all-to-all(f32[16,16,1280]{2,1,0:T(8,128)S(1)} %bitcast.37), channel_id=1, replica_groups=mesh['gx'=16,'gy'=8] {'gx'}, dimensions={0} | all-to-all | bytes 2621440 | tf_op jit(solution)/shard_map/all_to_all | solution.py:258
  148.7 22.6 %all_to_all.58 = f32[16,16,1280]{2,1,0:T(8,128)S(1)} all-to-all(f32[16,16,1280]{2,1,0:T(8,128)S(1)} %broadcast_in_dim.12), channel_id=1, replica_groups=mesh['gx'=16,'gy'=8] {'gx'}, dimensions={0} | all-to-all | bytes 2621440 | tf_op jit(solution)/shard_map/all_to_all | solution.py:263
  175.9 7.1 %shard_map.60 = f32[256,256]{1,0:T(8,128)S(1)} custom-call(f32[256,256]{1,0:T(8,128)S(1)} %slice.17.c_ref), custom_call_target="tpu_custom_call" | custom-call | flops 1073741824 | bytes 1048576 | tf_op jit(solution)/shard_map/pallas_call | solution.py:134
  187.7 23.2 %all_to_all.59 = f32[16,16,1280]{2,1,0:T(8,128)S(1)} all-to-all(f32[16,16,1280]{2,1,0:T(8,128)S(1)} %bitcast.38), channel_id=1, replica_groups=mesh['gx'=16,'gy'=8] {'gx'}, dimensions={0} | all-to-all | bytes 2621440 | tf_op jit(solution)/shard_map/all_to_all | solution.py:258
  211.1 22.6 %all_to_all.60 = f32[16,16,1280]{2,1,0:T(8,128)S(1)} all-to-all(f32[16,16,1280]{2,1,0:T(8,128)S(1)} %broadcast_in_dim.13), channel_id=1, replica_groups=mesh['gx'=16,'gy'=8] {'gx'}, dimensions={0} | all-to-all | bytes 2621440 | tf_op jit(solution)/shard_map/all_to_all | solution.py:263
  240.9 7.1 %shard_map.61 = f32[256,256]{1,0:T(8,128)S(1)} custom-call(f32[256,256]{1,0:T(8,128)S(1)} %slice.19.c_ref), custom_call_target="tpu_custom_call" | custom-call | flops 1073741824 | bytes 1048576 | tf_op jit(solution)/shard_map/pallas_call | solution.py:134
  250.4 11.9 %all_to_all.61 = f32[16,16,256]{2,1,0:T(8,128)S(1)} all-to-all(f32[16,16,256]{2,1,0:T(8,128)S(1)} %bitcast.43), channel_id=1, replica_groups=mesh['gx'=16,'gy'=8] {'gx'}, dimensions={0} | all-to-all | bytes 524288 | tf_op jit(solution)/shard_map/all_to_all | solution.py:258
  262.3 11.8 %all_to_all.62 = f32[16,16,256]{2,1,0:T(8,128)S(1)} all-to-all(f32[16,16,256]{2,1,0:T(8,128)S(1)} %broadcast_in_dim.14), channel_id=1, replica_groups=mesh['gx'=16,'gy'=8] {'gx'}, dimensions={0} | all-to-all | bytes 524288 | tf_op jit(solution)/shard_map/all_to_all | solution.py:263
  274.1 7.1 %shard_map.62 = f32[256,256]{1,0:T(8,128)S(1)} custom-call(f32[256,256]{1,0:T(8,128)S(1)} %bitcast.30), custom_call_target="tpu_custom_call" | custom-call | flops 1073741824 | bytes 1048576 | tf_op jit(solution)/shard_map/pallas_call | solution.py:134
  281.5 2.0 fusion.23
  283.6 3.8 %all-to-all-start.10 = ((f32[16,16,1024]{2,1,0:T(8,128)}), f32[16,16,1024]{2,1,0:T(8,128)S(1)}, u32[]{:S(2)}, u32[]{:S(2)}) async-start(f32[16,16,1024]{2,1,0:T(8,128)} %bitcast.12), calls=%async_computation.10 | async-start | bytes 2097152 | tf_op jit(solution)/shard_map/all_to_all | solution.py:258
  288.9 14.2 %all-to-all-done.10 = f32[16,16,1024]{2,1,0:T(8,128)S(1)} async-done(((f32[16,16,1024]{2,1,0:T(8,128)}), f32[16,16,1024]{2,1,0:T(8,128)S(1)}, u32[]{:S(2)}, u32[]{:S(2)}) %all-to-all-start.10) | async-done | bytes 1048608 | tf_op jit(solution)/shard_map/all_to_all | solution.py:258
  (85 shorter events, 37.3 us)
Async XLA Ops:
  9.8 31.0 %copy-start.3 = (f32[256,32]{0,1:T(8,128)S(1)}, f32[256,32]{0,1:T(8,128)}, u32[]{:S(2)}) copy-start(f32[256,32]{0,1:T(8,128)} %param.4) | copy-start | bytes 98308
  25.8 1.3 collective-permute-start
  27.0 5.9 %collective-permute-start.3 = (f32[16,256]{1,0:T(8,128)S(1)}, f32[16,256]{1,0:T(8,128)S(1)}, u32[]{:S(2)}, u32[]{:S(2)}) collective-permute-start(f32[16,256]{1,0:T(8,128)S(1)} %add.64), channel_id=1, source_target_pairs={{0,6},{1,7},{2,0},{3,1},{4,2},{5,3},{6,4},{7,5},{8,14},{9,15},{10,... | collective-permute-start | bytes 49160 | tf_op jit(solution)/shard_map/ppermute | solution.py:277
  31.1 4.9 %collective-permute-start.2 = (f32[16,256]{1,0:T(8,128)S(1)}, f32[16,256]{1,0:T(8,128)S(1)}, u32[]{:S(2)}, u32[]{:S(2)}) collective-permute-start(f32[16,256]{1,0:T(8,128)S(1)} %add.64), channel_id=1, source_target_pairs={{0,2},{1,3},{2,4},{3,5},{4,6},{5,7},{6,0},{7,1},{8,10},{9,11},{10,... | collective-permute-start | bytes 49160 | tf_op jit(solution)/shard_map/ppermute | solution.py:277
  31.1 5.2 %collective-permute-start.1 = (f32[16,256]{1,0:T(8,128)S(1)}, f32[16,256]{1,0:T(8,128)S(1)}, u32[]{:S(2)}, u32[]{:S(2)}) collective-permute-start(f32[16,256]{1,0:T(8,128)S(1)} %add.64), channel_id=1, source_target_pairs={{0,4},{1,5},{2,6},{3,7},{4,0},{5,1},{6,2},{7,3},{8,12},{9,13},{10,... | collective-permute-start | bytes 49160 | tf_op jit(solution)/shard_map/ppermute | solution.py:277
  37.1 12.4 %all-to-all-start.1 = ((f32[16,16,256]{2,1,0:T(8,128)}), f32[16,16,256]{2,1,0:T(8,128)S(1)}, u32[]{:S(2)}, u32[]{:S(2)}) async-start(f32[16,16,256]{2,1,0:T(8,128)} %broadcast_in_dim.10), calls=%async_computation.1 | async-start | bytes 524288 | tf_op jit(solution)/shard_map/all_to_all | solution.py:263
  89.3 18.5 %copy-start = (f32[256,1024]{1,0:T(8,128)S(1)}, f32[256,1024]{1,0:T(8,128)}, u32[]{:S(2)}) copy-start(f32[256,1024]{1,0:T(8,128)} %get-tuple-element.20) | copy-start | bytes 3145732
  89.3 18.5 %all-to-all-start.3 = ((f32[16,16,1024]{2,1,0:T(8,128)}), f32[16,16,1024]{2,1,0:T(8,128)S(1)}, u32[]{:S(2)}, u32[]{:S(2)}) async-start(f32[16,16,1024]{2,1,0:T(8,128)} %broadcast_in_dim.11), calls=%async_computation.3 | async-start | bytes 2097152 | tf_op jit(solution)/shard_map/all_to_all | solution.py:263
  108.9 1.4 collective-permute-start.4
  110.3 5.8 %collective-permute-start.7 = (f32[128,256]{1,0:T(8,128)S(1)}, f32[128,256]{1,0:T(8,128)S(1)}, u32[]{:S(2)}, u32[]{:S(2)}) collective-permute-start(f32[128,256]{1,0:T(8,128)S(1)} %dynamic-slice_add_fusion.2), channel_id=1, source_target_pairs={{0,6},{1,7},{2,0},{3,1},{4,2},{5,3},{6,4},{7,5},{8,14},{9,15},{10,... | collective-permute-start | bytes 393224 | tf_op jit(solution)/shard_map/ppermute | solution.py:291
  113.0 9.3 %collective-permute-start.6 = (f32[128,256]{1,0:T(8,128)S(1)}, f32[128,256]{1,0:T(8,128)S(1)}, u32[]{:S(2)}, u32[]{:S(2)}) collective-permute-start(f32[128,256]{1,0:T(8,128)S(1)} %dynamic-slice_add_fusion.2), channel_id=1, source_target_pairs={{0,2},{1,3},{2,4},{3,5},{4,6},{5,7},{6,0},{7,1},{8,10},{9,11},{10,... | collective-permute-start | bytes 393224 | tf_op jit(solution)/shard_map/ppermute | solution.py:291
  113.0 9.3 %collective-permute-start.5 = (f32[128,256]{1,0:T(8,128)S(1)}, f32[128,256]{1,0:T(8,128)S(1)}, u32[]{:S(2)}, u32[]{:S(2)}) collective-permute-start(f32[128,256]{1,0:T(8,128)S(1)} %dynamic-slice_add_fusion.2), channel_id=1, source_target_pairs={{0,4},{1,5},{2,6},{3,7},{4,0},{5,1},{6,2},{7,3},{8,12},{9,13},{10,... | collective-permute-start | bytes 393224 | tf_op jit(solution)/shard_map/ppermute | solution.py:291
  122.3 1.4 collective-permute-start.8
  172.3 1.4 collective-permute-start.9
  173.8 9.2 %collective-permute-start.12 = (f32[128,256]{1,0:T(8,128)S(1)}, f32[128,256]{1,0:T(8,128)S(1)}, u32[]{:S(2)}, u32[]{:S(2)}) collective-permute-start(f32[128,256]{1,0:T(8,128)S(1)} %dynamic-slice_add_fusion.1), channel_id=1, source_target_pairs={{0,6},{1,7},{2,0},{3,1},{4,2},{5,3},{6,4},{7,5},{8,14},{9,15},{10,... | collective-permute-start | bytes 393224 | tf_op jit(solution)/shard_map/ppermute | solution.py:291
  174.3 8.7 %collective-permute-start.11 = (f32[128,256]{1,0:T(8,128)S(1)}, f32[128,256]{1,0:T(8,128)S(1)}, u32[]{:S(2)}, u32[]{:S(2)}) collective-permute-start(f32[128,256]{1,0:T(8,128)S(1)} %dynamic-slice_add_fusion.1), channel_id=1, source_target_pairs={{0,4},{1,5},{2,6},{3,7},{4,0},{5,1},{6,2},{7,3},{8,12},{9,13},{10,... | collective-permute-start | bytes 393224 | tf_op jit(solution)/shard_map/ppermute | solution.py:291
  174.5 9.4 %collective-permute-start.10 = (f32[128,256]{1,0:T(8,128)S(1)}, f32[128,256]{1,0:T(8,128)S(1)}, u32[]{:S(2)}, u32[]{:S(2)}) collective-permute-start(f32[128,256]{1,0:T(8,128)S(1)} %dynamic-slice_add_fusion.1), channel_id=1, source_target_pairs={{0,2},{1,3},{2,4},{3,5},{4,6},{5,7},{6,0},{7,1},{8,10},{9,11},{10,... | collective-permute-start | bytes 393224 | tf_op jit(solution)/shard_map/ppermute | solution.py:291
  183.9 1.8 collective-permute-start.13
  234.7 1.4 collective-permute-start.14
  236.2 11.8 %collective-permute-start.17 = (f32[128,256]{1,0:T(8,128)S(1)}, f32[128,256]{1,0:T(8,128)S(1)}, u32[]{:S(2)}, u32[]{:S(2)}) collective-permute-start(f32[128,256]{1,0:T(8,128)S(1)} %dynamic-slice_add_fusion), channel_id=1, source_target_pairs={{0,6},{1,7},{2,0},{3,1},{4,2},{5,3},{6,4},{7,5},{8,14},{9,15},{10,... | collective-permute-start | bytes 393224 | tf_op jit(solution)/shard_map/ppermute | solution.py:291
  238.1 10.0 %collective-permute-start.16 = (f32[128,256]{1,0:T(8,128)S(1)}, f32[128,256]{1,0:T(8,128)S(1)}, u32[]{:S(2)}, u32[]{:S(2)}) collective-permute-start(f32[128,256]{1,0:T(8,128)S(1)} %dynamic-slice_add_fusion), channel_id=1, source_target_pairs={{0,4},{1,5},{2,6},{3,7},{4,0},{5,1},{6,2},{7,3},{8,12},{9,13},{10,... | collective-permute-start | bytes 393224 | tf_op jit(solution)/shard_map/ppermute | solution.py:291
  239.6 8.4 %collective-permute-start.15 = (f32[128,256]{1,0:T(8,128)S(1)}, f32[128,256]{1,0:T(8,128)S(1)}, u32[]{:S(2)}, u32[]{:S(2)}) collective-permute-start(f32[128,256]{1,0:T(8,128)S(1)} %dynamic-slice_add_fusion), channel_id=1, source_target_pairs={{0,2},{1,3},{2,4},{3,5},{4,6},{5,7},{6,0},{7,1},{8,10},{9,11},{10,... | collective-permute-start | bytes 393224 | tf_op jit(solution)/shard_map/ppermute | solution.py:291
  248.1 1.4 collective-permute-start.18
  283.6 19.5 %all-to-all-start.10 = ((f32[16,16,1024]{2,1,0:T(8,128)}), f32[16,16,1024]{2,1,0:T(8,128)S(1)}, u32[]{:S(2)}, u32[]{:S(2)}) async-start(f32[16,16,1024]{2,1,0:T(8,128)} %bitcast.12), calls=%async_computation.10 | async-start | bytes 2097152 | tf_op jit(solution)/shard_map/all_to_all | solution.py:258
  (2 other events, 4.5 us)

commit v3 on v2

--- a/solution.py
+++ b/solution.py
@@ -142,36 +142,36 @@
     )(c)
 
 
-def gram_kernel(m_ref, out_ref, high, cross, low):
-    step = pl.program_id(0)
-
-    @pl.when(step == 0)
-    def _():
-        high[...] = jnp.zeros_like(high)
-        cross[...] = jnp.zeros_like(cross)
-        low[...] = jnp.zeros_like(low)
-
-    h, l = split2(m_ref[...])
-    high[...] += dot(h, h, 0, 0)
-    cross[...] += dot(h, l, 0, 0)
-    low[...] += dot(l, l, 0, 0)
-
-    @pl.when(step == pl.num_programs(0) - 1)
-    def _():
-        c = cross[...]
-        out_ref[...] = high[...] + (c + c.T + low[...])
+CHUNKS = (512, 1536, 2048, 2048, 2048)
+
+
+def gram_kernel(m_hbm, out_ref, buf, sems):
+    copies, starts, at = [], [], 0
+    for i, rows in enumerate(CHUNKS):
+        span = pl.ds(at, rows)
+        copies.append(pltpu.make_async_copy(m_hbm.at[span], buf.at[span], sems.at[i]))
+        starts.append(at)
+        at += rows
+    for copy in copies:
+        copy.start()
+    high = cross = low = None
+    for copy, at, rows in zip(copies, starts, CHUNKS):
+        copy.wait()
+        h, l = split2(buf[at : at + rows, :])
+        hh, hl, ll = dot(h, h, 0, 0), dot(h, l, 0, 0), dot(l, l, 0, 0)
+        high, cross, low = (hh, hl, ll) if high is None else (high + hh, cross + hl, low + ll)
+    out_ref[...] = high + (cross + cross.T + low)
 
 
 def time_gram(field):
-    rows, n = field.shape
-    block = 1024
+    n = field.shape[1]
+    assert field.shape[0] == sum(CHUNKS)
     return pl.pallas_call(
         gram_kernel,
-        grid=(rows // block,),
         out_shape=jax.ShapeDtypeStruct((n, n), F32),
-        in_specs=[pl.BlockSpec((block, n), lambda i: (i, 0))],
-        out_specs=pl.BlockSpec((n, n), lambda i: (0, 0)),
-        scratch_shapes=[pltpu.VMEM((n, n), F32)] * 3,
+        in_specs=[pl.BlockSpec(memory_space=pl.ANY)],
+        out_specs=pl.BlockSpec(memory_space=pltpu.VMEM),
+        scratch_shapes=[pltpu.VMEM(field.shape, F32), pltpu.SemaphoreType.DMA((len(CHUNKS),))],
         compiler_params=pltpu.CompilerParams(vmem_limit_bytes=56 << 20),
     )(field)
 
@@ -190,13 +190,10 @@
     return dot6(inverse_factor(gram6(z)), split3(z)).T
 
 
-def project_kernel(g_ref, s_ref, u_ref, m_hbm, q_ref, shrunk_ref, v_ref, gs, m_left, m_right, weights, sems):
-    rows, n = m_hbm.shape
+def project_kernel(g_ref, s_ref, u_ref, m_hbm, q_ref, shrunk_ref, v_ref, gs, by_y, weights, sems):
+    cells_y = m_hbm.shape[1]
     lanes = 128
-    copies = [
-        pltpu.make_async_copy(m_hbm.at[:, pl.ds(i * lanes, lanes)], half, sems.at[i])
-        for i, half in enumerate((m_left, m_right))
-    ]
+    copies = [pltpu.make_async_copy(m_hbm.at[:, y, :], by_y.at[y], sems.at[y]) for y in range(cells_y)]
     for copy in copies:
         copy.start()
     q = time_steps(g_ref, s_ref, gs)
@@ -208,26 +205,22 @@
     for k in range(per):
         pad = lambda a: jnp.pad(a, ((0, 0), (k * rank, lanes - (k + 1) * rank)))
         weights[k] = jnp.concatenate([pad(qh), pad(ql)], axis=1).astype(BF16)
-    for copy in copies:
-        copy.wait()
-    cells_x = shrunk_ref.shape[0]
-    cells_y = rows // cells_x
     for group in range(cells_y // per):
-        wide = jnp.zeros((cells_x, 2 * lanes), F32)
-        thin = jnp.zeros((cells_x, lanes), F32)
+        wide = thin = None
         for k in range(per):
-            at = pl.ds(group * per + k, cells_x, stride=cells_y)
-            h, l = split2(jnp.concatenate([m_left[at, :], m_right[at, :]], axis=1))
-            wide = wide + dot(h, weights[k])
-            thin = thin + dot(l, weights[k, :, :lanes])
+            y = group * per + k
+            copies[y].wait()
+            h, l = split2(by_y[y])
+            a, b = dot(h, weights[k]), dot(l, weights[k, :, :lanes])
+            wide, thin = (a, b) if k == 0 else (wide + a, thin + b)
         shrunk_ref[:, group * lanes : (group + 1) * lanes] = wide[:, :lanes] + (wide[:, lanes:] + thin)
     v_ref[...] = jnp.dot(u_ref[...].T, shrunk_ref[...], precision=HI, preferred_element_type=F32)
 
 
-def project(gram, start_time, start_x, field, cells_x):
-    rows, n = field.shape
+def project(gram, start_time, start_x, field):
+    cells_x, cells_y, n = field.shape
     rank = start_time.shape[1]
-    cols = rows // cells_x * rank
+    cols = cells_y * rank
     vmem = pl.BlockSpec(memory_space=pltpu.VMEM)
     return pl.pallas_call(
         project_kernel,
@@ -240,10 +233,9 @@
         out_specs=(vmem, vmem, vmem),
         scratch_shapes=[
             pltpu.VMEM((3, n, n), BF16),
-            pltpu.VMEM((rows, n // 2), F32),
-            pltpu.VMEM((rows, n // 2), F32),
+            pltpu.VMEM((cells_y, cells_x, n), F32),
             pltpu.VMEM((128 // rank, n, 256), BF16),
-            pltpu.SemaphoreType.DMA((2,)),
+            pltpu.SemaphoreType.DMA((cells_y,)),
         ],
         compiler_params=pltpu.CompilerParams(vmem_limit_bytes=56 << 20),
     )(gram, start_time, start_x, field)
@@ -278,42 +270,46 @@
     return (p + got[1]) + (got[0] + got[2])
 
 
-def sum_gy(z, size, square=None):
-    swap, turns = gy_moves(size)
-    core = lax.axis_index("gy") % 2
-    half = z.shape[0] // 2
-    mine = lax.dynamic_slice_in_dim(z, core * half, half, 0)
-    other = lax.dynamic_slice_in_dim(z, (1 - core) * half, half, 0)
-    mine = mine + lax.ppermute(other, "gy", swap)
+def both_halves(mine, size):
+    rest = lax.ppermute(mine, "gy", gy_moves(size)[0])
+    first = lax.axis_index("gy") % 2 == 0
+    return jnp.concatenate([jnp.where(first, mine, rest), jnp.where(first, rest, mine)], axis=0)
+
+
+def sum_gy(part, size, square=None):
     inv = None
     if square is not None:
-        mine, square = lax.optimization_barrier((mine, square))
-    got = [lax.ppermute(mine, "gy", turn) for turn in turns]
+        part, square = lax.optimization_barrier((part, square))
+    got = [lax.ppermute(part, "gy", turn) for turn in gy_moves(size)[1]]
     if square is not None:
         got, inv = lax.optimization_barrier((got, chol_inverse(square)))
-    total = (mine + got[1]) + (got[0] + got[2])
-    rest = lax.ppermute(total, "gy", swap)
-    first = core == 0
-    full = jnp.concatenate([jnp.where(first, total, rest), jnp.where(first, rest, total)], axis=0)
-    return full, inv
+    return both_halves((part + got[1]) + (got[0] + got[2]), size), inv
 
 
 def local(melt_field, start_time, start_x, *, gx, gy):
     cells_x, cells_y, time_len = melt_field.shape
     field = melt_field.reshape(cells_x * cells_y, time_len)
     gram = spread(sum_gy_small(scatter_sum(time_gram(field), "gx", gx), gy), "gx", gx)
-    time_basis, shrunk, v = project(gram, start_time, start_x, field, cells_x)
-    cols = shrunk.shape[1]
+    core_id = lax.axis_index("gy") % 2
+    half = start_x.shape[1] // 2
+    start = lax.dynamic_slice_in_dim(start_x, core_id * half, half, 1)
+    time_basis, own, v = project(gram, start_time, start, melt_field)
+    other = lax.ppermute(own, "gy", gy_moves(gy)[0])
+    v = jnp.concatenate([v, precise(start.T, other, 0)], axis=1)
+    chip = jnp.concatenate([own, other], axis=1)
+    cols = chip.shape[1]
     v = spread(scatter_sum(v, "gx", gx), "gx", gx)
-    z, _ = sum_gy(precise(v, shrunk, 1), gy)
+    z, _ = sum_gy(precise(v, chip, 1), gy)
     for sweep in range(SWEEPS_X - 1):
-        vc = jnp.concatenate([precise(z, shrunk, 0), precise(z, z, 1)], axis=1)
+        mine = lax.dynamic_slice_in_dim(z, core_id * half, half, 0)
+        vc = jnp.concatenate([precise(mine, chip, 0), precise(mine, z, 1)], axis=1)
         vc = spread(scatter_sum(vc, "gx", gx), "gx", gx)
-        z, inv = sum_gy(precise(vc[:, :cols], shrunk, 1), gy, vc[:, cols:])
+        square = both_halves(vc[:, cols:], gy)
+        z, inv = sum_gy(precise(vc[:, :cols], chip, 1), gy, square)
         z = precise(inv, z, 0)
     inv = chol_inverse(spread(scatter_sum(precise(z, z, 1), "gx", gx), "gx", gx))
     u = precise(inv, z, 0)
-    core = scatter_sum(precise(u, shrunk, 0), "gx", gx)
+    core = scatter_sum(precise(u, own, 0), "gx", gx)
     return (time_basis, u.T, core)
 
 

time: 308 us -> 310 us (level)
  matrix products: 9.58 us -> 14.3 us
  Pallas kernels: 49.3 us -> 44.9 us
  local copies, waits for them, and re-layouts: 5.19 us -> 9.28 us
  blocking collectives: 150 us -> 146 us
  waiting for transfers between devices: 57.8 us -> 53.8 us
    dot_general x12 -> x13, matrix products: 9.58 us -> 14.3 us  [precise(): lax.dot_general(a, b, (((1,), (cb,)), ((), ())), precision=HI, preferred_...]
    ppermute x15, waiting for transfers between devices: 16.6 us -> 12.8 us  [the longest x9 5.97 us: sum_gy(): got = [lax.ppermute(part, 'gy', turn) for turn in gy_moves(size)[1]]]
  transfers between devices with their start and end apart: 22 -> 22, of which waited for: 15 -> 12; matrix products, arithmetic and copies ran while one was open for 1% -> 3% of each run, Pallas kernels for 5% -> 5%
where the time goes in v3:
time: 310 us; the launch traced here: 304 us
  blocking collectives  146 us (47%)
  waiting for transfers between devices  53.8 us (17%)
  Pallas kernels  44.9 us (14%)
  starting transfers between devices  31 us (10%)
  matrix products  14.3 us (5%)
  local copies, waits for them, and re-layouts  9.28 us (3%)
  other arithmetic  3.73 us (1%)
    all_to_all x5, blocking collectives, scatter_sum(): return jnp.sum(lax.all_to_all(parts, axis, 0, 0, tiled=True), axis=0)  91.9 us
    all_to_all x3, blocking collectives, spread(): got = lax.all_to_all(copies, axis, 0, 0, tiled=True)  54.2 us
    all_to_all x2, waiting for transfers between devices, spread(): got = lax.all_to_all(copies, axis, 0, 0, tiled=True)  22.1 us
    pallas_call x3, Pallas kernels, chol_inverse(): pl.pallas_call(chol_kernel, out_shape=jax.ShapeDtypeStruct((n, n), F32),...  21.2 us
    pallas_call x1, Pallas kernels, project(): pl.pallas_call(project_kernel, out_shape=(jax.ShapeDtypeStruct((n, rank),...  15.9 us
    dot_general x13, matrix products, precise(): lax.dot_general(a, b, (((1,), (cb,)), ((), ())), precision=HI, preferred_...  14.3 us
    all_to_all x1, waiting for transfers between devices, scatter_sum(): return jnp.sum(lax.all_to_all(parts, axis, 0, 0, tiled=True), axis=0)  14.2 us
    ppermute x9, starting transfers between devices, sum_gy(): got = [lax.ppermute(part, 'gy', turn) for turn in gy_moves(size)[1]]  12.9 us
  transfers between devices with their start and end apart: 22, of which 12 were waited for; matrix products, arithmetic and copies ran while one was open for 3% of the time, Pallas kernels for 5%

profile of v3, /device:TPU:0, one launch (start us, length us, event | category | flops | bytes accessed | tf_op | source)
XLA Modules:
  0.0 304.3 jit_solution(6439615882417864946)
XLA Ops:
  0.7 7.8 %shard_map.58 = f32[256,256]{1,0:T(8,128)} custom-call(f32[8192,256]{1,0:T(8,128)} %bitcast.35), custom_call_target="tpu_custom_call" | custom-call | tf_op jit(solution)/shard_map/pallas_call | solution.py:169
  8.5 15.8 %all_to_all.55 = f32[16,16,256]{2,1,0:T(8,128)S(1)} all-to-all(f32[16,16,256]{2,1,0:T(8,128)} %bitcast.44), channel_id=1, replica_groups=mesh['gx'=16,'gy'=8] {'gx'}, dimensions={0} | all-to-all | bytes 524288 | tf_op jit(solution)/shard_map/all_to_all | solution.py:250
  31.5 3.5 %collective-permute-done.1 = f32[16,256]{1,0:T(8,128)S(1)} collective-permute-done((f32[16,256]{1,0:T(8,128)S(1)}, f32[16,256]{1,0:T(8,128)S(1)}, u32[]{:S(2)}, u32[]{:S(2)}) %collective-permute-start.1) | collective-permute-done | bytes 16416 | tf_op jit(solution)/shard_map/ppermute | solution.py:269
  35.7 3.7 %all-to-all-start.1 = ((f32[16,16,256]{2,1,0:T(8,128)}), f32[16,16,256]{2,1,0:T(8,128)S(1)}, u32[]{:S(2)}, u32[]{:S(2)}) async-start(f32[16,16,256]{2,1,0:T(8,128)} %broadcast_in_dim.10), calls=%async_computation.1 | async-start | bytes 524288 | tf_op jit(solution)/shard_map/all_to_all | solution.py:255
  40.8 7.2 %all-to-all-done.1 = f32[16,16,256]{2,1,0:T(8,128)S(1)} async-done(((f32[16,16,256]{2,1,0:T(8,128)}), f32[16,16,256]{2,1,0:T(8,128)S(1)}, u32[]{:S(2)}, u32[]{:S(2)}) %all-to-all-start.1) | async-done | bytes 262176 | tf_op jit(solution)/shard_map/all_to_all | solution.py:255
  48.7 15.9 %shard_map.59 = (f32[256,32]{1,0:T(8,128)}, f32[256,1024]{1,0:T(8,128)}, f32[128,1024]{1,0:T(8,128)}) custom-call(f32[256,256]{1,0:T(8,128)} %bitcast.43, f32[256,32]{1,0:T(8,128)} %copy.6.s_ref, f32[256,128]{1,0:T(8,128)} %constant_dynamic-slice_fusion.u_ref, f32[256,32,256]{2,1,0:T(8,128)} %m_hbm.1), custom_call_target="tpu_custom_call" | custom-call | tf_op jit(solution)/shard_map/pallas_call | solution.py:225
  64.7 2.9 collective-permute-done.4
  69.7 20.4 %all_to_all.56 = f32[16,8,2048]{2,1,0:T(8,128)S(1)} all-to-all(f32[16,8,2048]{2,1,0:T(8,128)S(1)} %maximum_bitcast_fusion.2), channel_id=1, replica_groups=mesh['gx'=16,'gy'=8] {'gx'}, dimensions={0} | all-to-all | bytes 2097152 | tf_op jit(solution)/shard_map/all_to_all | solution.py:250
  91.2 3.7 %all-to-all-start.3 = ((f32[16,8,2048]{2,1,0:T(8,128)}), f32[16,8,2048]{2,1,0:T(8,128)S(1)}, u32[]{:S(2)}, u32[]{:S(2)}) async-start(f32[16,8,2048]{2,1,0:T(8,128)} %broadcast_in_dim.11), calls=%async_computation.3 | async-start | bytes 2097152 | tf_op jit(solution)/shard_map/all_to_all | solution.py:255
  96.5 14.9 %all-to-all-done.3 = f32[16,8,2048]{2,1,0:T(8,128)S(1)} async-done(((f32[16,8,2048]{2,1,0:T(8,128)}), f32[16,8,2048]{2,1,0:T(8,128)S(1)}, u32[]{:S(2)}, u32[]{:S(2)}) %all-to-all-start.3) | async-done | bytes 1048608 | tf_op jit(solution)/shard_map/all_to_all | solution.py:255
  113.6 3.2 %collective-permute-start.7 = (f32[128,256]{1,0:T(8,128)S(1)}, f32[128,256]{1,0:T(8,128)S(1)}, u32[]{:S(2)}, u32[]{:S(2)}) collective-permute-start(f32[128,256]{1,0:T(8,128)S(1)} %fusion.4), channel_id=1, source_target_pairs={{0,6},{1,7},{2,0},{3,1},{4,2},{5,3},{6,4},{7,5},{8,14},{9,15},{10,... | collective-permute-start | bytes 393224 | tf_op jit(solution)/shard_map/ppermute | solution.py:283
  117.4 3.2 %collective-permute-done.6 = f32[128,256]{1,0:T(8,128)S(1)} collective-permute-done((f32[128,256]{1,0:T(8,128)S(1)}, f32[128,256]{1,0:T(8,128)S(1)}, u32[]{:S(2)}, u32[]{:S(2)}) %collective-permute-start.6) | collective-permute-done | bytes 131104 | tf_op jit(solution)/shard_map/ppermute | solution.py:283
  126.8 21.7 %all_to_all.57 = f32[16,8,2304]{2,1,0:T(8,128)S(1)} all-to-all(f32[16,8,2304]{2,1,0:T(8,128)S(1)} %maximum_bitcast_fusion), channel_id=1, replica_groups=mesh['gx'=16,'gy'=8] {'gx'}, dimensions={0} | all-to-all | bytes 2359296 | tf_op jit(solution)/shard_map/all_to_all | solution.py:250
  150.2 21.2 %all_to_all.58 = f32[16,8,2304]{2,1,0:T(8,128)S(1)} all-to-all(f32[16,8,2304]{2,1,0:T(8,128)S(1)} %broadcast_in_dim.12), channel_id=1, replica_groups=mesh['gx'=16,'gy'=8] {'gx'}, dimensions={0} | all-to-all | bytes 2359296 | tf_op jit(solution)/shard_map/all_to_all | solution.py:255
  174.6 3.1 %collective-permute-start.11 = (f32[128,256]{1,0:T(8,128)S(1)}, f32[128,256]{1,0:T(8,128)S(1)}, u32[]{:S(2)}, u32[]{:S(2)}) collective-permute-start(f32[128,256]{1,0:T(8,128)S(1)} %fusion.2), channel_id=1, source_target_pairs={{0,4},{1,5},{2,6},{3,7},{4,0},{5,1},{6,2},{7,3},{8,12},{9,13},{10,... | collective-permute-start | bytes 393224 | tf_op jit(solution)/shard_map/ppermute | solution.py:283
  177.7 7.1 %shard_map.60 = f32[256,256]{1,0:T(8,128)S(1)} custom-call(f32[256,256]{1,0:T(8,128)S(1)} %pad_maximum_fusion.2.c_ref), custom_call_target="tpu_custom_call" | custom-call | flops 1073741824 | bytes 1048576 | tf_op jit(solution)/shard_map/pallas_call | solution.py:134
  188.9 21.9 %all_to_all.59 = f32[16,8,2304]{2,1,0:T(8,128)S(1)} all-to-all(f32[16,8,2304]{2,1,0:T(8,128)S(1)} %maximum_bitcast_fusion.1), channel_id=1, replica_groups=mesh['gx'=16,'gy'=8] {'gx'}, dimensions={0} | all-to-all | bytes 2359296 | tf_op jit(solution)/shard_map/all_to_all | solution.py:250
  212.4 21.2 %all_to_all.60 = f32[16,8,2304]{2,1,0:T(8,128)S(1)} all-to-all(f32[16,8,2304]{2,1,0:T(8,128)S(1)} %broadcast_in_dim.13), channel_id=1, replica_groups=mesh['gx'=16,'gy'=8] {'gx'}, dimensions={0} | all-to-all | bytes 2359296 | tf_op jit(solution)/shard_map/all_to_all | solution.py:255
  241.2 7.1 %shard_map.61 = f32[256,256]{1,0:T(8,128)S(1)} custom-call(f32[256,256]{1,0:T(8,128)S(1)} %pad_maximum_fusion.3.c_ref), custom_call_target="tpu_custom_call" | custom-call | flops 1073741824 | bytes 1048576 | tf_op jit(solution)/shard_map/pallas_call | solution.py:134
  250.6 12.1 %all_to_all.61 = f32[16,16,256]{2,1,0:T(8,128)S(1)} all-to-all(f32[16,16,256]{2,1,0:T(8,128)S(1)} %bitcast.45), channel_id=1, replica_groups=mesh['gx'=16,'gy'=8] {'gx'}, dimensions={0} | all-to-all | bytes 524288 | tf_op jit(solution)/shard_map/all_to_all | solution.py:250
  262.7 11.8 %all_to_all.62 = f32[16,16,256]{2,1,0:T(8,128)S(1)} all-to-all(f32[16,16,256]{2,1,0:T(8,128)S(1)} %broadcast_in_dim.14), channel_id=1, replica_groups=mesh['gx'=16,'gy'=8] {'gx'}, dimensions={0} | all-to-all | bytes 524288 | tf_op jit(solution)/shard_map/all_to_all | solution.py:255
  274.5 7.1 %shard_map.62 = f32[256,256]{1,0:T(8,128)S(1)} custom-call(f32[256,256]{1,0:T(8,128)S(1)} %bitcast.34), custom_call_target="tpu_custom_call" | custom-call | flops 1073741824 | bytes 1048576 | tf_op jit(solution)/shard_map/pallas_call | solution.py:134
  284.0 3.7 %all-to-all-start.10 = ((f32[16,16,1024]{2,1,0:T(8,128)}), f32[16,16,1024]{2,1,0:T(8,128)S(1)}, u32[]{:S(2)}, u32[]{:S(2)}) async-start(f32[16,16,1024]{2,1,0:T(8,128)} %bitcast.12), calls=%async_computation.10 | async-start | bytes 2097152 | tf_op jit(solution)/shard_map/all_to_all | solution.py:250
  289.2 14.2 %all-to-all-done.10 = f32[16,16,1024]{2,1,0:T(8,128)S(1)} async-done(((f32[16,16,1024]{2,1,0:T(8,128)}), f32[16,16,1024]{2,1,0:T(8,128)S(1)}, u32[]{:S(2)}, u32[]{:S(2)}) %all-to-all-start.10) | async-done | bytes 1048608 | tf_op jit(solution)/shard_map/all_to_all | solution.py:250
  (96 shorter events, 48.9 us)
Async XLA Ops:
  0.6 39.5 %copy-start = (f32[256,256]{1,0:T(8,128)S(1)}, f32[256,256]{1,0:T(8,128)}, u32[]{:S(2)}) copy-start(f32[256,256]{1,0:T(8,128)} %param.5) | copy-start | bytes 786436
  0.6 38.7 %copy-start.7 = (f32[256,32]{0,1:T(8,128)S(1)}, f32[256,32]{0,1:T(8,128)}, u32[]{:S(2)}) copy-start(f32[256,32]{0,1:T(8,128)} %param.4) | copy-start | bytes 98308
  24.3 1.3 collective-permute-start
  25.6 5.9 %collective-permute-start.2 = (f32[16,256]{1,0:T(8,128)S(1)}, f32[16,256]{1,0:T(8,128)S(1)}, u32[]{:S(2)}, u32[]{:S(2)}) collective-permute-start(f32[16,256]{1,0:T(8,128)S(1)} %add.53), channel_id=1, source_target_pairs={{0,2},{1,3},{2,4},{3,5},{4,6},{5,7},{6,0},{7,1},{8,10},{9,11},{10,... | collective-permute-start | bytes 49160 | tf_op jit(solution)/shard_map/ppermute | solution.py:269
  27.5 4.0 %collective-permute-start.3 = (f32[16,256]{1,0:T(8,128)S(1)}, f32[16,256]{1,0:T(8,128)S(1)}, u32[]{:S(2)}, u32[]{:S(2)}) collective-permute-start(f32[16,256]{1,0:T(8,128)S(1)} %add.53), channel_id=1, source_target_pairs={{0,6},{1,7},{2,0},{3,1},{4,2},{5,3},{6,4},{7,5},{8,14},{9,15},{10,... | collective-permute-start | bytes 49160 | tf_op jit(solution)/shard_map/ppermute | solution.py:269
  29.7 5.2 %collective-permute-start.1 = (f32[16,256]{1,0:T(8,128)S(1)}, f32[16,256]{1,0:T(8,128)S(1)}, u32[]{:S(2)}, u32[]{:S(2)}) collective-permute-start(f32[16,256]{1,0:T(8,128)S(1)} %add.53), channel_id=1, source_target_pairs={{0,4},{1,5},{2,6},{3,7},{4,0},{5,1},{6,2},{7,3},{8,12},{9,13},{10,... | collective-permute-start | bytes 49160 | tf_op jit(solution)/shard_map/ppermute | solution.py:269
  35.7 12.4 %all-to-all-start.1 = ((f32[16,16,256]{2,1,0:T(8,128)}), f32[16,16,256]{2,1,0:T(8,128)S(1)}, u32[]{:S(2)}, u32[]{:S(2)}) async-start(f32[16,16,256]{2,1,0:T(8,128)} %broadcast_in_dim.10), calls=%async_computation.1 | async-start | bytes 524288 | tf_op jit(solution)/shard_map/all_to_all | solution.py:255
  64.6 3.0 collective-permute-start.4
  91.2 20.1 %all-to-all-start.3 = ((f32[16,8,2048]{2,1,0:T(8,128)}), f32[16,8,2048]{2,1,0:T(8,128)S(1)}, u32[]{:S(2)}, u32[]{:S(2)}) async-start(f32[16,8,2048]{2,1,0:T(8,128)} %broadcast_in_dim.11), calls=%async_computation.3 | async-start | bytes 2097152 | tf_op jit(solution)/shard_map/all_to_all | solution.py:255
  113.6 7.1 %collective-permute-start.6 = (f32[128,256]{1,0:T(8,128)S(1)}, f32[128,256]{1,0:T(8,128)S(1)}, u32[]{:S(2)}, u32[]{:S(2)}) collective-permute-start(f32[128,256]{1,0:T(8,128)S(1)} %fusion.4), channel_id=1, source_target_pairs={{0,2},{1,3},{2,4},{3,5},{4,6},{5,7},{6,0},{7,1},{8,10},{9,11},{10,... | collective-permute-start | bytes 393224 | tf_op jit(solution)/shard_map/ppermute | solution.py:283
  113.6 7.1 %collective-permute-start.7 = (f32[128,256]{1,0:T(8,128)S(1)}, f32[128,256]{1,0:T(8,128)S(1)}, u32[]{:S(2)}, u32[]{:S(2)}) collective-permute-start(f32[128,256]{1,0:T(8,128)S(1)} %fusion.4), channel_id=1, source_target_pairs={{0,6},{1,7},{2,0},{3,1},{4,2},{5,3},{6,4},{7,5},{8,14},{9,15},{10,... | collective-permute-start | bytes 393224 | tf_op jit(solution)/shard_map/ppermute | solution.py:283
  116.9 6.5 %collective-permute-start.5 = (f32[128,256]{1,0:T(8,128)S(1)}, f32[128,256]{1,0:T(8,128)S(1)}, u32[]{:S(2)}, u32[]{:S(2)}) collective-permute-start(f32[128,256]{1,0:T(8,128)S(1)} %fusion.4), channel_id=1, source_target_pairs={{0,4},{1,5},{2,6},{3,7},{4,0},{5,1},{6,2},{7,3},{8,12},{9,13},{10,... | collective-permute-start | bytes 393224 | tf_op jit(solution)/shard_map/ppermute | solution.py:283
  123.4 1.6 collective-permute-start.8
  171.4 2.3 collective-permute-start.9
  173.8 11.0 %collective-permute-start.10 = (f32[128,256]{1,0:T(8,128)S(1)}, f32[128,256]{1,0:T(8,128)S(1)}, u32[]{:S(2)}, u32[]{:S(2)}) collective-permute-start(f32[128,256]{1,0:T(8,128)S(1)} %fusion.2), channel_id=1, source_target_pairs={{0,2},{1,3},{2,4},{3,5},{4,6},{5,7},{6,0},{7,1},{8,10},{9,11},{10,... | collective-permute-start | bytes 393224 | tf_op jit(solution)/shard_map/ppermute | solution.py:283
  174.6 10.2 %collective-permute-start.11 = (f32[128,256]{1,0:T(8,128)S(1)}, f32[128,256]{1,0:T(8,128)S(1)}, u32[]{:S(2)}, u32[]{:S(2)}) collective-permute-start(f32[128,256]{1,0:T(8,128)S(1)} %fusion.2), channel_id=1, source_target_pairs={{0,4},{1,5},{2,6},{3,7},{4,0},{5,1},{6,2},{7,3},{8,12},{9,13},{10,... | collective-permute-start | bytes 393224 | tf_op jit(solution)/shard_map/ppermute | solution.py:283
  177.7 7.1 %collective-permute-start.12 = (f32[128,256]{1,0:T(8,128)S(1)}, f32[128,256]{1,0:T(8,128)S(1)}, u32[]{:S(2)}, u32[]{:S(2)}) collective-permute-start(f32[128,256]{1,0:T(8,128)S(1)} %fusion.2), channel_id=1, source_target_pairs={{0,6},{1,7},{2,0},{3,1},{4,2},{5,3},{6,4},{7,5},{8,14},{9,15},{10,... | collective-permute-start | bytes 393224 | tf_op jit(solution)/shard_map/ppermute | solution.py:283
  184.9 1.8 collective-permute-start.13
  233.7 2.3 collective-permute-start.14
  236.1 12.2 %collective-permute-start.15 = (f32[128,256]{1,0:T(8,128)S(1)}, f32[128,256]{1,0:T(8,128)S(1)}, u32[]{:S(2)}, u32[]{:S(2)}) collective-permute-start(f32[128,256]{1,0:T(8,128)S(1)} %fusion), channel_id=1, source_target_pairs={{0,2},{1,3},{2,4},{3,5},{4,6},{5,7},{6,0},{7,1},{8,10},{9,11},{10,... | collective-permute-start | bytes 393224 | tf_op jit(solution)/shard_map/ppermute | solution.py:283
  238.2 10.1 %collective-permute-start.16 = (f32[128,256]{1,0:T(8,128)S(1)}, f32[128,256]{1,0:T(8,128)S(1)}, u32[]{:S(2)}, u32[]{:S(2)}) collective-permute-start(f32[128,256]{1,0:T(8,128)S(1)} %fusion), channel_id=1, source_target_pairs={{0,4},{1,5},{2,6},{3,7},{4,0},{5,1},{6,2},{7,3},{8,12},{9,13},{10,... | collective-permute-start | bytes 393224 | tf_op jit(solution)/shard_map/ppermute | solution.py:283
  239.9 8.4 %collective-permute-start.17 = (f32[128,256]{1,0:T(8,128)S(1)}, f32[128,256]{1,0:T(8,128)S(1)}, u32[]{:S(2)}, u32[]{:S(2)}) collective-permute-start(f32[128,256]{1,0:T(8,128)S(1)} %fusion), channel_id=1, source_target_pairs={{0,6},{1,7},{2,0},{3,1},{4,2},{5,3},{6,4},{7,5},{8,14},{9,15},{10,... | collective-permute-start | bytes 393224 | tf_op jit(solution)/shard_map/ppermute | solution.py:283
  248.3 1.4 collective-permute-start.18
  284.0 19.4 %all-to-all-start.10 = ((f32[16,16,1024]{2,1,0:T(8,128)}), f32[16,16,1024]{2,1,0:T(8,128)S(1)}, u32[]{:S(2)}, u32[]{:S(2)}) async-start(f32[16,16,1024]{2,1,0:T(8,128)} %bitcast.12), calls=%async_computation.10 | async-start | bytes 2097152 | tf_op jit(solution)/shard_map/all_to_all | solution.py:250
  (6 other events, 35.3 us)
